TPU v7x, 128 devices: a whole 4x4x4 slice. The times are simulated.
128 devices in a mesh: row: 4 (over z), col: 32 (over x, y, core).
Axes of the slice: x: 4, y: 4, z: 4, core: 2. Of those that a mesh axis runs over, the one named last changes fastest.
Arguments:
- scan: float32 [4096, 32768], P('row', 'col'), may hold values from -6 to 6
- anchors: int32 [2, 8, 32, 2], P(None, 'row', 'col'), may hold values from -1 to 32256, as said below
- targets: int32 [2, 8, 32], P(None, 'row', 'col'), may hold values from 0 to 8
- stem_weight: bfloat16 [7, 7, 1, 64], replicated, may hold values from -0.875 to 0.875
- stem_bias: float32 [64], replicated, may hold values from -3 to 3
- conv1_weight: bfloat16 [3, 3, 64, 64], replicated, may hold values from -0.25 to 0.25
- conv1_bias: float32 [64], replicated, may hold values from -3 to 3
- conv2_weight: bfloat16 [3, 3, 64, 64], replicated, may hold values from -0.25 to 0.25
- conv2_bias: float32 [64], replicated, may hold values from -3 to 3
- head_weight: bfloat16 [64, 9], replicated, may hold values from -0.75 to 0.75
- head_bias: float32 [9], replicated, may hold values from -4 to 4
Outputs:
- saliency: float32 [4096, 32768], P('row', 'col')
- class_scores: float32 [2, 8, 32], P(None, 'row', 'col')
Inputs may be any that keep to these rules, and one draw needn't show every extreme that they name: anchors[p, k, c] is the top-left corner (row, column) of a window lying wholly inside the scan, or has row -1 when the slot is empty. Slots r * 2 to (r + 1) * 2 - 1 of tile column c hold only windows whose corner lies in tile (r, c), that is rows r * 1024 to (r + 1) * 1024 - 1 and columns c * 1024 to (c + 1) * 1024 - 1. In every pass some tile holds 2 live windows and some tile column holds 4; no tile column holds more than 4 live windows in a pass. Every tile column has empty slots in every pass, and empty slots have column c * 1024 + 512.
All inputs are finite; a program needn't handle non-finite values.
Results may differ from a plain program's by a relative error of at most 0.0054.
Values may be sent and summed in bfloat16 or wider, within the bound.
A program may use at most 192 MiB of HBM per device.

v0:
```python
import jax
import jax.numpy as jnp
from jax import lax
from jax.sharding import PartitionSpec as P

WIN = 512
CLASSES = 9


def shifted(shard, axis, by):
    devices = lax.axis_size(axis)
    pairs = [(i, i + by) for i in range(devices) if 0 <= i + by < devices]
    return lax.ppermute(shard, axis, pairs)


def convolve(inputs, kernel, stride, margin):
    result = lax.conv_general_dilated(
        inputs[None],
        kernel,
        (stride, stride),
        ((margin, margin), (margin, margin)),
        dimension_numbers=("NHWC", "HWIO", "NHWC"),
        preferred_element_type=jnp.float32,
    )
    return result[0]


def turned(kernel):
    return jnp.flip(kernel, (0, 1)).transpose(0, 1, 3, 2)


def gaussian(offset):
    centre = (WIN - 1) / 2.0
    sigma = WIN / 4.0
    return jnp.exp(-((offset - centre) ** 2) / (2.0 * sigma * sigma))


def explain(
    cutout,
    target,
    stem_weight,
    stem_bias,
    conv1_weight,
    conv1_bias,
    conv2_weight,
    conv2_bias,
    head_weight,
    head_bias,
):
    stem_map = jax.nn.relu(convolve(cutout[:, :, None], stem_weight, 2, 3) + stem_bias).astype(
        jnp.bfloat16
    )
    features_a = lax.reduce_window(
        stem_map,
        jnp.array(-jnp.inf, jnp.bfloat16),
        lax.max,
        (3, 3, 1),
        (2, 2, 1),
        ((1, 1), (1, 1), (0, 0)),
    )
    pre_first = convolve(features_a, conv1_weight, 1, 1) + conv1_bias
    hidden = jax.nn.relu(pre_first).astype(jnp.bfloat16)
    pre_second = features_a.astype(jnp.float32) + convolve(hidden, conv2_weight, 1, 1) + conv2_bias
    activated = jax.nn.relu(pre_second)
    features = jnp.mean(activated, (0, 1))
    onehot = (jnp.arange(CLASSES, dtype=jnp.int32) == target).astype(jnp.float32)
    head_matrix = head_weight.astype(jnp.float32)
    logits = jnp.dot(features, head_matrix, precision=lax.Precision.HIGHEST) + head_bias
    class_logit = jnp.sum(logits * onehot)
    column = jnp.dot(head_matrix, onehot, precision=lax.Precision.HIGHEST)
    side = WIN // 4
    grad_out = (jnp.where(pre_second > 0, column, 0.0) / float(side * side)).astype(jnp.bfloat16)
    grad_hidden = convolve(grad_out, turned(conv2_weight), 1, 1)
    grad_pre = jnp.where(pre_first > 0, grad_hidden, 0.0).astype(jnp.bfloat16)
    grad_input = grad_out.astype(jnp.float32) + convolve(grad_pre, turned(conv1_weight), 1, 1)
    channel_weights = jnp.sum(grad_input, (0, 1))
    class_map = jax.nn.relu(
        jnp.einsum(
            "ijk,k->ij",
            features_a.astype(jnp.float32),
            channel_weights,
            precision=lax.Precision.HIGHEST,
        )
    )
    upsampled = jnp.repeat(jnp.repeat(class_map, 4, 0), 4, 1)
    profile = gaussian(jnp.arange(WIN, dtype=jnp.int32).astype(jnp.float32))
    return (upsampled * profile[:, None] * profile[None, :], class_logit)


def run_windows(source, top_rows, left_cols, is_live, slot_targets, network):
    crop_count = top_rows.shape[0]

    def compute(window_px, target):
        return explain(window_px, target, *network)

    def empty(window_px, target):
        return (jnp.zeros((WIN, WIN), jnp.float32), jnp.zeros((), jnp.float32))

    def handle(number, carried):
        contribs, scores = carried
        start_row = jnp.where(is_live[number], top_rows[number], 0)
        start_col = jnp.where(is_live[number], left_cols[number], 0)
        cutout = lax.dynamic_slice(source, (start_row, start_col), (WIN, WIN))
        contrib, class_logit = lax.cond(
            is_live[number], compute, empty, cutout, slot_targets[number]
        )
        contribs = lax.dynamic_update_slice(contribs, contrib[None], (number, 0, 0))
        scores = lax.dynamic_update_slice(scores, class_logit[None], (number,))
        return (contribs, scores)

    blank_contribs = jnp.zeros((crop_count, WIN, WIN), jnp.float32)
    blank_scores = jnp.zeros((crop_count,), jnp.float32)
    return lax.fori_loop(0, crop_count, handle, (blank_contribs, blank_scores))


def local(
    scan,
    anchors,
    targets,
    stem_weight,
    stem_bias,
    conv1_weight,
    conv1_bias,
    conv2_weight,
    conv2_bias,
    head_weight,
    head_bias,
):
    network = (
        stem_weight,
        stem_bias,
        conv1_weight,
        conv1_bias,
        conv2_weight,
        conv2_bias,
        head_weight,
        head_bias,
    )
    tile_size = scan.shape[0]
    row_index = lax.axis_index("row")
    col_index = lax.axis_index("col")
    pixels = scan.astype(jnp.bfloat16)
    corners_flat = anchors.reshape(1, -1)
    targets_flat = targets.reshape(1, -1)
    every_corner, every_target = (
        lax.all_gather(corners_flat, ("row", "col"), axis=0, tiled=True),
        lax.all_gather(targets_flat, ("row", "col"), axis=0, tiled=True),
    )
    corner_list = every_corner.reshape(-1, 2)
    live_all = corner_list[:, 0] >= 0
    row_pixels = row_index * tile_size + jnp.arange(tile_size, dtype=jnp.int32)
    col_pixels = col_index * tile_size + jnp.arange(tile_size, dtype=jnp.int32)

    def spread(positions, starts):
        offset = positions[:, None] - starts[None, :]
        inside = live_all[None, :] & (offset >= 0) & (offset < WIN)
        return jnp.where(inside, gaussian(offset.astype(jnp.float32)), 0.0)

    weights_sum = jnp.dot(
        spread(row_pixels, corner_list[:, 0]),
        spread(col_pixels, corner_list[:, 1]).T,
        precision=lax.Precision.HIGHEST,
    )
    lower_rim = shifted(pixels[:WIN, :], "row", -1)
    stacked = jnp.concatenate([pixels, lower_rim], 0)
    right_rim = shifted(stacked[:, :WIN], "col", -1)
    framed = jnp.concatenate([stacked, right_rim], 1)
    corners = anchors.reshape(-1, 2)
    is_live = corners[:, 0] >= 0
    top_rows = corners[:, 0] - row_index * tile_size
    left_cols = corners[:, 1] - col_index * tile_size
    contribs, scores = run_windows(
        framed, top_rows, left_cols, is_live, targets.reshape(-1), network
    )

    def deposit(number, canvas):
        start_row = jnp.where(is_live[number], top_rows[number], 0)
        start_col = jnp.where(is_live[number], left_cols[number], 0)
        existing = lax.dynamic_slice(canvas, (start_row, start_col), (WIN, WIN))
        return lax.dynamic_update_slice(canvas, existing + contribs[number], (start_row, start_col))

    blank_canvas = jnp.zeros((tile_size + WIN, tile_size + WIN), jnp.float32)
    canvas = lax.fori_loop(0, contribs.shape[0], deposit, blank_canvas)
    returned = shifted(canvas[:, tile_size:], "col", 1)
    left_part = canvas[:, :tile_size]
    left_part = jnp.concatenate([left_part[:, :WIN] + returned, left_part[:, WIN:]], 1)
    bottom_rows = shifted(left_part[tile_size:, :], "row", 1)
    upper_part = left_part[:tile_size]
    summed = jnp.concatenate([upper_part[:WIN] + bottom_rows, upper_part[WIN:]], 0)
    class_scores = scores.reshape(targets.shape)
    saliency = summed / jnp.maximum(weights_sum, 1.0)
    return (saliency, class_scores)


def solution(mesh):
    placed = (
        P("row", "col"),
        P(None, "row", "col", None),
        P(None, "row", "col"),
        P(),
        P(),
        P(),
        P(),
        P(),
        P(),
        P(),
        P(),
    )
    return jax.shard_map(
        local,
        mesh=mesh,
        in_specs=placed,
        out_specs=(P("row", "col"), P(None, "row", "col")),
        check_vma=False,
    )
```

profile of v0, /device:TPU:36, one launch (start us, length us, event | category | flops | bytes accessed | tf_op | source)
XLA Modules:
  0.0 1444.2 jit_solution(8979350367818175760)
XLA Ops:
  6.2 25.0 %collective-permute-done = bf16[512,1024]{0,1:T(8,128)(2,1)S(1)} collective-permute-done((bf16[512,1024]{0,1:T(8,128)(2,1)S(1)}, bf16[512,1024]{0,1:T(8,128)(2,1)S(1)}, u32[]{:S(2)}, u32[]{:S(2)}) %collective-permute-start) | collective-permute-done | bytes 1048608 | tf_op jit(solution)/shard_map/ppermute | solution.py:13
  38.7 15.6 %collective-permute-done.1 = bf16[1536,512]{0,1:T(8,128)(2,1)} collective-permute-done((bf16[1536,512]{0,1:T(8,128)(2,1)}, bf16[1536,512]{0,1:T(8,128)(2,1)}, u32[]{:S(2)}, u32[]{:S(2)}) %collective-permute-start.1) | collective-permute-done | bytes 1572896 | tf_op jit(solution)/shard_map/ppermute | solution.py:13
  61.8 804.7 %while.28 = (s32[]{:T(128)}, f32[4,512,512]{1,2,0:T(8,128)}, f32[4]{0:T(128)}, pred[4]{0:T(512)(128)(4,1)}, s32[4]{0:T(128)}, /*index=5*/s32[4]{0:T(128)S(1)}, s...) while((s32[]{:T(128)}, f32[4,512,512]{1,2,0:T(8,128)}, ...), condition=%wide.region_7.8_spmd, body=%wide.region_0.7_spmd.sunk | while | flops 5642895872 | bytes 216064592 | solution.py:113
  74.3 379.2 %conditional.2 = (f32[]{:T(128)}, f32[1,512,512]{1,2,0:T(8,128)}) conditional(s32[]{:T(128)} %convert_element_type.145, () %tuple.93, (s32[4]{0:T(128)}, s32[]{:T(128)}, s32[4]{0:T(128)S(1)}, pred[]{:T(512)}, s32[4]{0:T(128)S(1)}, /*index=5*/bf16[1536,1536]{0,1:T(8,128)(2,1)}, bf16[7,7,1,64]{3,2,1,0:T(2,128)(2,1)S(1)}, f32[64]{0:T(128)}, ...), branch_computations={%region_1.1_spmd, %region_2.6_spmd} | conditional | flops 5642895872 | bytes 213966464 | solution.py:104
  80.1 23.1 %copy.43 = bf16[512,8,72,1]{1,3,2,0:T(2,128)(2,1)} copy(bf16[512,8,72,1]{0,2,3,1:T(8,128)(2,1)S(1)} %fusion.66) | data formatting | bytes 1179648 | tf_op jit(solution)/shard_map/while/body/eval_jaxpr/cond/branch_1_fun/conv_general_dilated | solution.py:17
  103.1 135.1 %broadcast_select_fusion = f32[256,8,33,64]{3,1,2,0:T(8,128)} fusion(pred[8,33]{0,1:T(8,128)(4,1)S(1)} %copy-done.19, bf16[512,8,72,1]{1,3,2,0:T(2,128)(2,1)} %copy.43, bf16[7,7,1,64]{3,2,1,0:T(2,128)(2,1)S(1)} %get-tuple-element.483), kind=kOutput, calls=%fused_computation | convolution fusion | flops 426792960 | bytes 17897864 | tf_op jit(solution)/shard_map/while/body/eval_jaxpr/cond/branch_1_fun/conv_general_dilated | solution.py:17
  238.3 27.8 %copy.44 = f32[256,8,33,64]{0,3,2,1:T(8,128)} copy(f32[256,8,33,64]{3,1,2,0:T(8,128)} %broadcast_select_fusion) | data formatting | bytes 34603008 | tf_op jit(solution)/shard_map/while/body/eval_jaxpr/cond/branch_1_fun/conv_general_dilated | solution.py:17
  266.1 9.9 fusion.2
  275.9 73.8 %reduce_window.8 = bf16[128,128,64]{0,2,1:T(8,128)(2,1)S(1)} reduce-window(bf16[256,256,64]{0,2,1:T(8,128)(2,1)} %fusion.2, bf16[]{:T(256)} %constant.110.clone), window={size=3x3x1 stride=2x2x1 pad=1_1x1_1x0_0}, to_apply=%region_3.2 | reduce-window | flops 8388608 | bytes 10485762 | tf_op jit(solution)/shard_map/while/body/eval_jaxpr/cond/branch_1_fun/reduce_window | solution.py:53
  351.6 8.6 copy.46
  373.2 8.6 fusion.20
  381.9 9.1 copy.47
  407.1 14.5 %fusion.48 = bf16[128,1,8,17,64]{4,2,3,0,1:T(8,128)(2,1)S(1)} fusion(f32[128,8,17,64]{3,1,2,0:T(8,128)} %copy-done, f32[64]{0:T(128)S(1)} %copy-done.10, pred[8,17]{0,1:T(8,128)(4,1)S(1)} %copy-done.4, bf16[3,3,64,64]{3,2,1,0:T(8,128)(2,1)S(1)} %copy-done.13, bf16[128,1,7,2,64]{4,2,3,0,1:T(8,128)(2,1)S(1)} %slice.72, bf16[128,1,8,17,64]{4,2,3,0,1:T(8,128)(2,1)} %copy.49), kind=kOutput, calls=%fused_computation.52 | convolution fusion | flops 1292042240 | bytes 9216392 | tf_op jit(solution)/shard_map/while/body/eval_jaxpr/cond/branch_1_fun/conv_general_dilated | solution.py:17
  421.7 13.1 fusion.25
  434.8 9.1 copy.50
  464.3 379.6 %conditional.2 = (f32[]{:T(128)}, f32[1,512,512]{1,2,0:T(8,128)}) conditional(s32[]{:T(128)} %convert_element_type.145, () %tuple.93, (s32[4]{0:T(128)}, s32[]{:T(128)}, s32[4]{0:T(128)S(1)}, pred[]{:T(512)}, s32[4]{0:T(128)S(1)}, /*index=5*/bf16[1536,1536]{0,1:T(8,128)(2,1)}, bf16[7,7,1,64]{3,2,1,0:T(2,128)(2,1)S(1)}, f32[64]{0:T(128)}, ...), branch_computations={%region_1.1_spmd, %region_2.6_spmd} | conditional | flops 5642895872 | bytes 213966464 | solution.py:104
  470.0 23.1 %copy.43 = bf16[512,8,72,1]{1,3,2,0:T(2,128)(2,1)} copy(bf16[512,8,72,1]{0,2,3,1:T(8,128)(2,1)S(1)} %fusion.66) | data formatting | bytes 1179648 | tf_op jit(solution)/shard_map/while/body/eval_jaxpr/cond/branch_1_fun/conv_general_dilated | solution.py:17
  493.1 135.1 %broadcast_select_fusion = f32[256,8,33,64]{3,1,2,0:T(8,128)} fusion(pred[8,33]{0,1:T(8,128)(4,1)S(1)} %copy-done.19, bf16[512,8,72,1]{1,3,2,0:T(2,128)(2,1)} %copy.43, bf16[7,7,1,64]{3,2,1,0:T(2,128)(2,1)S(1)} %get-tuple-element.483), kind=kOutput, calls=%fused_computation | convolution fusion | flops 426792960 | bytes 17897864 | tf_op jit(solution)/shard_map/while/body/eval_jaxpr/cond/branch_1_fun/conv_general_dilated | solution.py:17
  628.3 27.9 %copy.44 = f32[256,8,33,64]{0,3,2,1:T(8,128)} copy(f32[256,8,33,64]{3,1,2,0:T(8,128)} %broadcast_select_fusion) | data formatting | bytes 34603008 | tf_op jit(solution)/shard_map/while/body/eval_jaxpr/cond/branch_1_fun/conv_general_dilated | solution.py:17
  656.2 9.9 fusion.2
  666.1 73.8 %reduce_window.8 = bf16[128,128,64]{0,2,1:T(8,128)(2,1)S(1)} reduce-window(bf16[256,256,64]{0,2,1:T(8,128)(2,1)} %fusion.2, bf16[]{:T(256)} %constant.110.clone), window={size=3x3x1 stride=2x2x1 pad=1_1x1_1x0_0}, to_apply=%region_3.2 | reduce-window | flops 8388608 | bytes 10485762 | tf_op jit(solution)/shard_map/while/body/eval_jaxpr/cond/branch_1_fun/reduce_window | solution.py:53
  741.7 8.6 copy.46
  763.4 8.6 fusion.20
  772.0 9.1 copy.47
  797.3 14.5 %fusion.48 = bf16[128,1,8,17,64]{4,2,3,0,1:T(8,128)(2,1)S(1)} fusion(f32[128,8,17,64]{3,1,2,0:T(8,128)} %copy-done, f32[64]{0:T(128)S(1)} %copy-done.10, pred[8,17]{0,1:T(8,128)(4,1)S(1)} %copy-done.4, bf16[3,3,64,64]{3,2,1,0:T(8,128)(2,1)S(1)} %copy-done.13, bf16[128,1,7,2,64]{4,2,3,0,1:T(8,128)(2,1)S(1)} %slice.72, bf16[128,1,8,17,64]{4,2,3,0,1:T(8,128)(2,1)} %copy.49), kind=kOutput, calls=%fused_computation.52 | convolution fusion | flops 1292042240 | bytes 9216392 | tf_op jit(solution)/shard_map/while/body/eval_jaxpr/cond/branch_1_fun/conv_general_dilated | solution.py:17
  811.9 13.2 fusion.25
  825.0 9.1 copy.50
  871.3 63.7 %while.29 = (s32[]{:T(128)}, f32[1536,1536]{1,0:T(8,128)}, pred[4]{0:T(512)(128)(4,1)}, s32[4]{0:T(128)S(1)}, s32[4]{0:T(128)S(1)}, /*index=5*/f32[4,512,512]{1,...) while((s32[]{:T(128)}, f32[1536,1536]{1,0:T(8,128)}, pred[4]{0:T(512)(128)(4,1)}, s32[4]{0:T(128)S(1)}, ...), condition=%wide.region_9.10_spmd, body=%wide.region_8.9_spmd.sunk | while | flops 262154 | bytes 9437425 | solution.py:183
  939.1 38.8 %collective-permute-done.2 = f32[1536,512]{1,0:T(8,128)S(1)} collective-permute-done((f32[1536,512]{1,0:T(8,128)S(1)}, f32[1536,512]{1,0:T(8,128)S(1)}, u32[]{:S(2)}, u32[]{:S(2)}) %collective-permute-start.2) | collective-permute-done | bytes 3145760 | tf_op jit(solution)/shard_map/ppermute | solution.py:13
  984.3 9.1 collective-permute-start.3
  994.0 434.1 %all-gather = s32[128,1,8]{2,1,0:T(1,128)S(1)} all-gather(s32[1,1,8]{2,1,0:T(1,128)S(1)} %reshape.171), channel_id=1, replica_groups=mesh['row'=4,'col'=32] {'row','col'}, dimensions={0}, use_global_device_ids=true | all-gather | bytes 4128 | tf_op jit(solution)/shard_map/all_gather | solution.py:146
  1432.8 10.8 fusion.93
  (210 shorter events, 209.8 us)
Async XLA Ops:
  4.0 32.1 %copy-start.6 = (s32[2,2,1,2]{3,2,1,0:T(1,128)S(1)}, s32[2,2,1,2]{3,2,1,0:T(1,128)}, u32[]{:S(2)}) copy-start(s32[2,2,1,2]{3,2,1,0:T(1,128)} %param.18) | copy-start | bytes 100
  4.0 32.8 %copy-start.11 = (s32[2,2,1]{1,2,0:T(1,128)S(1)}, s32[2,2,1]{1,2,0:T(1,128)}, u32[]{:S(2)}) copy-start(s32[2,2,1]{1,2,0:T(1,128)} %param.19) | copy-start | bytes 52
  4.0 34.1 %copy-start.8 = (bf16[7,7,1,64]{3,1,2,0:T(8,128)(2,1)S(1)}, bf16[7,7,1,64]{3,1,2,0:T(8,128)(2,1)}, u32[]{:S(2)}) copy-start(bf16[7,7,1,64]{3,1,2,0:T(8,128)(2,1)} %param.20) | copy-start | bytes 18820
  4.1 27.0 %collective-permute-start = (bf16[512,1024]{0,1:T(8,128)(2,1)S(1)}, bf16[512,1024]{0,1:T(8,128)(2,1)S(1)}, u32[]{:S(2)}, u32[]{:S(2)}) collective-permute-start(bf16[512,1024]{0,1:T(8,128)(2,1)S(1)} %slice.76), channel_id=1, source_target_pairs={{32,0},{64,32},{96,64},{33,1},{65,33},{97,65},{34,2},{66,34},{98,6... | collective-permute-start | bytes 3145736 | tf_op jit(solution)/shard_map/ppermute | solution.py:13
  32.4 21.9 %collective-permute-start.1 = (bf16[1536,512]{0,1:T(8,128)(2,1)}, bf16[1536,512]{0,1:T(8,128)(2,1)}, u32[]{:S(2)}, u32[]{:S(2)}) collective-permute-start(bf16[1536,512]{0,1:T(8,128)(2,1)} %pad_maximum_fusion.1), channel_id=1, source_target_pairs={{1,0},{2,1},{3,2},{4,3},{5,4},{6,5},{7,6},{8,7},{9,8},{10,9},{11,1... | collective-permute-start | bytes 4718600 | tf_op jit(solution)/shard_map/ppermute | solution.py:13
  63.9 7.8 copy-start.16
  74.3 381.5 %copy-start.16 = (f32[4]{0:T(128)S(1)}, f32[4]{0:T(128)}, u32[]{:S(2)}) copy-start(f32[4]{0:T(128)} %get-tuple-element.834) | copy-start | bytes 52 | tf_op jit(solution)/shard_map/while
  80.0 23.1 %copy-start.19 = (pred[8,33]{0,1:T(8,128)(4,1)S(1)}, pred[8,33]{0,1:T(8,128)(4,1)}, u32[]{:S(2)}) copy-start(pred[8,33]{0,1:T(8,128)(4,1)} %constant.152) | copy-start | bytes 796 | tf_op jit(solution)/shard_map/while/body/eval_jaxpr/cond
  238.3 27.8 %copy-start.9 = (f32[64]{0:T(128)S(1)}, f32[64]{0:T(128)}, u32[]{:S(2)}) copy-start(f32[64]{0:T(128)} %get-tuple-element.484) | copy-start | bytes 772 | tf_op jit(solution)/shard_map/while/body/eval_jaxpr/cond
  351.6 9.8 copy-start.12
  361.4 8.3 copy-start.4
  361.4 8.3 copy-start.10
  369.7 3.4 copy-start
  369.7 3.5 copy-start.13
  381.9 9.1 copy-start.15
  381.9 9.8 copy-start.3
  381.9 10.5 copy-start.5
  464.3 381.9 %copy-start.16 = (f32[4]{0:T(128)S(1)}, f32[4]{0:T(128)}, u32[]{:S(2)}) copy-start(f32[4]{0:T(128)} %get-tuple-element.834) | copy-start | bytes 52 | tf_op jit(solution)/shard_map/while
  470.0 23.1 %copy-start.19 = (pred[8,33]{0,1:T(8,128)(4,1)S(1)}, pred[8,33]{0,1:T(8,128)(4,1)}, u32[]{:S(2)}) copy-start(pred[8,33]{0,1:T(8,128)(4,1)} %constant.152) | copy-start | bytes 796 | tf_op jit(solution)/shard_map/while/body/eval_jaxpr/cond
  628.3 27.9 %copy-start.9 = (f32[64]{0:T(128)S(1)}, f32[64]{0:T(128)}, u32[]{:S(2)}) copy-start(f32[64]{0:T(128)} %get-tuple-element.484) | copy-start | bytes 772 | tf_op jit(solution)/shard_map/while/body/eval_jaxpr/cond
  741.7 9.8 copy-start.12
  751.5 8.3 copy-start.4
  751.5 8.3 copy-start.10
  759.9 3.5 copy-start.13
  772.0 9.1 copy-start.15
  772.0 9.8 copy-start.3
  772.0 10.5 copy-start.5
  854.4 7.8 copy-start.16
  937.2 40.7 %collective-permute-start.2 = (f32[1536,512]{1,0:T(8,128)S(1)}, f32[1536,512]{1,0:T(8,128)S(1)}, u32[]{:S(2)}, u32[]{:S(2)}) collective-permute-start(f32[1536,512]{1,0:T(8,128)S(1)} %slice.49), channel_id=1, source_target_pairs={{0,1},{1,2},{2,3},{3,4},{4,5},{5,6},{6,7},{7,8},{8,9},{9,10},{10,1... | collective-permute-start | bytes 9437192 | tf_op jit(solution)/shard_map/ppermute | solution.py:13
  981.9 11.4 copy-start.7
  981.9 447.4 %copy-start.18 = (f32[4]{0:T(128)S(1)}, f32[4]{0:T(128)}, u32[]{:S(2)}) copy-start(f32[4]{0:T(128)} %get-tuple-element.524) | copy-start | bytes 52
  984.3 445.7 %collective-permute-start.3 = (f32[512,1024]{1,0:T(8,128)}, f32[512,1024]{1,0:T(8,128)}, u32[]{:S(2)}, u32[]{:S(2)}) collective-permute-start(f32[512,1024]{1,0:T(8,128)} %fusion.108), channel_id=1, source_target_pairs={{0,32},{32,64},{64,96},{1,33},{33,65},{65,97},{2,34},{34,66},{66,9... | collective-permute-start | bytes 6291464 | tf_op jit(solution)/shard_map/ppermute | solution.py:13
  (9 other events, 16.6 us)
where the time goes:
time: 1470 us; the launch traced here: 1440 us
  blocking collectives  434 us (30%)
  matrix products  376 us (26%)
  local copies, waits for them, and re-layouts  277 us (19%)
  other arithmetic  214 us (15%)
  waiting for transfers between devices  79.3 us (5%)
  loops' own time  45.2 us (3%)
  starting transfers between devices  16.6 us (1%)
    all_gather x1, blocking collectives, local(): lax.all_gather(corners_flat, ('row', 'col'), axis=0, tiled=True)  434 us
    conv_general_dilated x10, matrix products, convolve(): lax.conv_general_dilated(inputs[None], kernel, (stride, stride), ((margin...  359 us
    conv_general_dilated x20, local copies, waits for them, and re-layouts, convolve(): lax.conv_general_dilated(inputs[None], kernel, (stride, stride), ((margin...  177 us
    another operation x2, other arithmetic, explain(): lax.reduce_window(stem_map, jnp.array(-jnp.inf, jnp.bfloat16), lax.max, (...  148 us
    ppermute x4, waiting for transfers between devices, shifted(): return lax.ppermute(shard, axis, pairs)  79.3 us
  transfers between devices with their start and end apart: 4, of which 3 were waited for; matrix products, arithmetic and copies ran while one was open for 0% of the time, Pallas kernels for 0%

commit v1 on v0

v1 whole, which is shorter than its diff:
```python
import jax
import jax.numpy as jnp
from jax import lax
from jax.experimental import pallas as pl
from jax.experimental.pallas import tpu as pltpu
from jax.sharding import PartitionSpec as P

WIN = 512
C = 64
F = 128
LOW = -3.0e38


def arranged(stem_weight, conv1_weight, conv2_weight):
    rows = jnp.arange(8)[:, None, None] * 2 + jnp.arange(7)[None, None, :]
    row_tap = (rows == jnp.arange(24)[None, :, None]).astype(jnp.float32)
    cols = jnp.arange(2)[:, None, None] * 2 + jnp.arange(7)[None, None, :]
    col_tap = (cols == jnp.arange(9)[None, :, None]).astype(jnp.float32)
    kernel = stem_weight[:, :, 0, :].astype(jnp.float32)
    part = jnp.einsum("rty,yxo->rtxo", row_tap, kernel)
    stem = jnp.einsum("qux,rtxo->rqout", col_tap, part)
    stem = stem.reshape(8 * 2 * C, 9 * 24).astype(jnp.bfloat16)
    first = conv1_weight.transpose(0, 3, 1, 2).reshape(3 * C, 3 * C)
    second = conv2_weight.transpose(0, 3, 1, 2).reshape(3 * C, 3 * C)
    back = jnp.flip(conv2_weight, (0, 1)).transpose(0, 2, 1, 3).reshape(3 * C, 3 * C)
    sums = jnp.flip(conv1_weight, (0, 1)).transpose(0, 1, 3, 2).reshape(9, C, C)
    return stem, first, second, back, sums.astype(jnp.float32)


def lanes(shape):
    return lax.broadcasted_iota(jnp.int32, shape, len(shape) - 1)


def put_taps(ref, row, value):
    lane = lanes((C, F))
    left = jnp.where(lane == 0, 0.0, pltpu.roll(value, 1, 1))
    right = jnp.where(lane == F - 1, 0.0, pltpu.roll(value, F - 1, 1))
    ref[row, 0:C, :] = left.astype(jnp.bfloat16)
    ref[row, C : 2 * C, :] = value.astype(jnp.bfloat16)
    ref[row, 2 * C : 3 * C, :] = right.astype(jnp.bfloat16)


def convolved(taps_ref, weight_ref, finish, state):
    weight = weight_ref[...]
    zero = jnp.zeros((C, F), jnp.float32)

    def four(step, carried):
        near, far, state = carried
        base = step * 4
        data = jnp.concatenate([taps_ref[base + k] for k in range(4)], 1)
        out = jnp.dot(weight, data, preferred_element_type=jnp.float32)
        part = lambda tap, k: out[tap * C : (tap + 1) * C, k * F : (k + 1) * F]
        state = finish(state, base - 1, near + part(2, 0))
        state = finish(state, base, far + part(1, 0) + part(2, 1))
        state = finish(state, base + 1, part(0, 0) + part(1, 1) + part(2, 2))
        state = finish(state, base + 2, part(0, 1) + part(1, 2) + part(2, 3))
        return part(0, 2) + part(1, 3), part(0, 3), state

    near, _, state = lax.fori_loop(0, F // 4, four, (zero, zero, state))
    return finish(state, F - 1, near)


def net_kernel(
    info, source, stem_w, first_w, second_w, back_w, sums_w, biases, heads, head_bias,
    map_ref, logit_ref,
    pixels, spread_ref, picked, feats, hidden, grads, edge, acc, arrival,
):
    slot = pl.program_id(0)
    live = info[slot, 0]
    top = info[slot, 1]
    left = info[slot, 2]
    target = info[slot, 3]

    @pl.when(live == 0)
    def _():
        map_ref[...] = jnp.zeros_like(map_ref)
        logit_ref[...] = jnp.zeros_like(logit_ref)

    @pl.when(live != 0)
    def _():
        row0 = pl.multiple_of(top // 16 * 16, 16)
        col0 = pl.multiple_of(left // 128 * 128, 128)
        copy = pltpu.make_async_copy(
            source.at[pl.ds(row0, 528), pl.ds(col0, 640)], pixels, arrival
        )
        copy.start()
        for u in range(9):
            at = lax.broadcasted_iota(jnp.int32, (640, F), 0) - (left - col0)
            want = lanes((640, F)) * 4 + (u - 3)
            hit = (at == want) & (want >= 0) & (want < WIN)
            spread_ref[:, u * F : (u + 1) * F] = jnp.where(hit, 1.0, 0.0).astype(jnp.bfloat16)
        row = lax.broadcasted_iota(jnp.int32, (520, 528), 0) - 3
        shift = jnp.where(
            (lanes((520, 528)) - (top - row0) == row) & (row >= 0) & (row < WIN), 1.0, 0.0
        ).astype(jnp.bfloat16)
        copy.wait()
        moved = jnp.dot(shift, pixels[...], preferred_element_type=jnp.float32)
        picked[...] = jnp.dot(
            moved.astype(jnp.bfloat16), spread_ref[...], preferred_element_type=jnp.float32
        )
        edge[...] = jnp.full_like(edge, LOW)
        stem_bias = biases[0]
        lane0 = lanes((C, F)) == 0

        def stem(step, _):
            slabs = []
            for k in range(2):
                start = pl.multiple_of((step * 2 + k) * 16, 16)
                slab = [
                    picked[pl.ds(start, 24), u * F : (u + 1) * F] for u in range(9)
                ]
                slabs.append(jnp.concatenate(slab, 0))
            data = jnp.concatenate(slabs, 1).astype(jnp.bfloat16)
            out = jnp.dot(stem_w[...], data, preferred_element_type=jnp.float32)
            even, odd = edge[0], edge[1]
            for k in range(2):
                for r in range(4):
                    part = lambda n: out[
                        (r * 4 + n) * C : (r * 4 + n + 1) * C, k * F : (k + 1) * F
                    ]
                    e_high = jnp.maximum(jnp.maximum(even, part(0)), part(2))
                    o_high = jnp.maximum(jnp.maximum(odd, part(1)), part(3))
                    even, odd = part(2), part(3)
                    before = jnp.where(lane0, LOW, pltpu.roll(o_high, 1, 1))
                    high = jnp.maximum(jnp.maximum(e_high, o_high), before)
                    high = jnp.maximum(high + stem_bias, 0.0)
                    put_taps(feats, step * 8 + k * 4 + r, high)
            edge[0] = even
            edge[1] = odd
            return 0

        lax.fori_loop(0, F // 8, stem, 0)

        def after_first(state, row, sums):
            row = jnp.maximum(row, 0)
            put_taps(hidden, row, jnp.maximum(sums + biases[1], 0.0))
            return state

        convolved(feats, first_w, after_first, 0)

        head = jnp.where(lanes((C, F)) == target, heads[...], 0.0)
        column = jnp.sum(head, 1, keepdims=True)
        grad = jnp.broadcast_to(
            (column / float(F * F)).astype(jnp.bfloat16).astype(jnp.float32), (C, F)
        )
        acc[...] = jnp.zeros_like(acc)

        def after_second(state, row, sums):
            keep = jnp.where(row >= 0, 1.0, 0.0)
            row = jnp.maximum(row, 0)
            value = sums + feats[row, C : 2 * C, :].astype(jnp.float32) + biases[2]
            value = jnp.maximum(value, 0.0)
            out = jnp.where(value > 0, grad, 0.0)
            acc[0] += value * keep
            acc[1] += out * keep
            put_taps(grads, row, out)
            return state

        convolved(hidden, second_w, after_second, 0)

        def after_back(state, row, sums):
            keep = jnp.where(row >= 0, 1.0, 0.0)
            row = jnp.maximum(row, 0)
            open_ = hidden[row, C : 2 * C, :].astype(jnp.float32) > 0
            value = jnp.where(open_, sums, 0.0).astype(jnp.bfloat16).astype(jnp.float32)
            acc[2] += value * keep
            acc[3] = jnp.where(row == 0, value, acc[3])
            acc[4] = value
            return state

        convolved(grads, back_w, after_back, 0)

        mean = jnp.sum(acc[0], 1, keepdims=True) / float(F * F)
        logit = jnp.sum(mean * column)
        bias = jnp.sum(jnp.where(lanes((1, F)) == target, head_bias[...], 0.0))
        logit_ref[...] = jnp.full((1, 8, F), logit + bias, jnp.float32)

        whole = acc[2]
        parts = [whole - acc[4], whole, whole - acc[3]]
        weights = jnp.zeros((1, C), jnp.float32)
        lane = lanes((C, F))
        for dy in range(3):
            for dx in range(3):
                drop = {0: F - 1, 1: F, 2: 0}[dx]
                total = jnp.sum(jnp.where(lane == drop, 0.0, parts[dy]), 1, keepdims=True)
                weights += jnp.sum(sums_w[dy * 3 + dx] * total, 0, keepdims=True)
        eye = lax.broadcasted_iota(jnp.int32, (C, C), 0) == lanes((C, C))
        channel = jnp.sum(jnp.where(eye, weights, 0.0), 1, keepdims=True)
        channel = channel + jnp.sum(acc[1], 1, keepdims=True)
        channel = jnp.broadcast_to(channel, (C, F))

        def rows(step, _):
            base = pl.multiple_of(step * 8, 8)
            found = [
                jnp.sum(
                    feats[base + k, C : 2 * C, :].astype(jnp.float32) * channel, 0, keepdims=True
                )
                for k in range(8)
            ]
            map_ref[0, pl.ds(base, 8), :] = jnp.maximum(jnp.concatenate(found, 0), 0.0)
            return 0

        lax.fori_loop(0, F // 8, rows, 0)


def networks(source, info, stem_weight, stem_bias, conv1_weight, conv1_bias, conv2_weight,
             conv2_bias, head_weight, head_bias):
    slots = info.shape[0]
    stem, first, second, back, sums = arranged(stem_weight, conv1_weight, conv2_weight)
    biases = jnp.broadcast_to(
        jnp.stack([stem_bias, conv1_bias, conv2_bias])[:, :, None], (3, C, F)
    )
    heads = jnp.pad(head_weight.astype(jnp.float32), ((0, 0), (0, F - 9)))
    bias_row = jnp.pad(head_bias[None], ((0, 0), (0, F - 9)))
    whole = pl.BlockSpec(memory_space=pltpu.VMEM)
    maps, logits = pl.pallas_call(
        net_kernel,
        grid_spec=pltpu.PrefetchScalarGridSpec(
            num_scalar_prefetch=1,
            grid=(slots,),
            in_specs=[pl.BlockSpec(memory_space=pl.ANY)] + [whole] * 8,
            out_specs=[
                pl.BlockSpec((1, F, F), lambda i, info: (i, 0, 0)),
                pl.BlockSpec((1, 8, F), lambda i, info: (i, 0, 0)),
            ],
            scratch_shapes=[
                pltpu.VMEM((528, 640), jnp.bfloat16),
                pltpu.VMEM((640, 9 * F), jnp.bfloat16),
                pltpu.VMEM((520, 9 * F), jnp.float32),
                pltpu.VMEM((F, 3 * C, F), jnp.bfloat16),
                pltpu.VMEM((F, 3 * C, F), jnp.bfloat16),
                pltpu.VMEM((F, 3 * C, F), jnp.bfloat16),
                pltpu.VMEM((2, C, F), jnp.float32),
                pltpu.VMEM((5, C, F), jnp.float32),
                pltpu.SemaphoreType.DMA,
            ],
        ),
        out_shape=[
            jax.ShapeDtypeStruct((slots, F, F), jnp.float32),
            jax.ShapeDtypeStruct((slots, 8, F), jnp.float32),
        ],
        compiler_params=pltpu.CompilerParams(vmem_limit_bytes=56 << 20),
    )(info, source, stem, first, second, back, sums, biases, heads, bias_row)
    return maps, logits[:, 0, 0]


def blend_kernel(info, maps, out_ref, below):
    size = out_ref.shape[0]
    out_ref[...] = jnp.zeros_like(out_ref)
    below[...] = jnp.zeros_like(below)

    def profile(offset):
        value = (offset - (WIN - 1) / 2.0) * (1.0 / (WIN / 4.0))
        return jnp.exp(-0.5 * value * value)

    def window(number, _):
        top = info[number, 1]
        left = info[number, 2]

        @pl.when(info[number, 0] != 0)
        def _():
            row0 = pl.multiple_of(jnp.clip(top // 8 * 8, 0, size - 520), 8)
            col0 = pl.multiple_of(jnp.clip(left // 128 * 128, 0, size - 640), 128)
            row = lax.broadcasted_iota(jnp.int32, (520, F), 0) + (row0 - top)
            in_row = (row >= 0) & (row < WIN)
            up = jnp.where(in_row & (row // 4 == lanes((520, F))), 1.0, 0.0)
            down = jnp.where(in_row, profile(row.astype(jnp.float32)), 0.0)
            col = lanes((F, 640)) + (col0 - left)
            in_col = (col >= 0) & (col < WIN)
            tap = lax.broadcasted_iota(jnp.int32, (F, 640), 0)
            across = jnp.where(in_col & (col // 4 == tap), 1.0, 0.0).astype(jnp.bfloat16)
            col = lanes((8, 640)) + (col0 - left)
            in_col = (col >= 0) & (col < WIN)
            side = jnp.where(in_col, profile(col.astype(jnp.float32)), 0.0)[0:1]
            tall = jnp.dot(
                up.astype(jnp.bfloat16), maps[number], preferred_element_type=jnp.float32
            ).astype(jnp.bfloat16)
            for k in range(5):
                part = slice(k * F, (k + 1) * F)
                at = (pl.ds(row0, 520), pl.ds(pl.multiple_of(col0 + k * F, F), F))
                weight = down * side[:, part]
                value = jnp.dot(tall, across[:, part], preferred_element_type=jnp.float32)
                out_ref[at] += value * weight
                below[at] += weight
        return 0

    lax.fori_loop(0, info.shape[0], window, 0)
    out_ref[...] = out_ref[...] / jnp.maximum(below[...], 1.0)


def blend(info, maps, size):
    return pl.pallas_call(
        blend_kernel,
        grid_spec=pltpu.PrefetchScalarGridSpec(
            num_scalar_prefetch=1,
            grid=(1,),
            in_specs=[pl.BlockSpec(memory_space=pltpu.VMEM)],
            out_specs=pl.BlockSpec((size, size), lambda i, info: (0, 0)),
            scratch_shapes=[pltpu.VMEM((size, size), jnp.float32)],
        ),
        out_shape=jax.ShapeDtypeStruct((size, size), jnp.float32),
        compiler_params=pltpu.CompilerParams(vmem_limit_bytes=40 << 20),
    )(info, maps)


def moved(shard, down, right):
    rows, cols = lax.axis_size("row"), lax.axis_size("col")
    pairs = [
        (r * cols + c, (r + down) * cols + c + right)
        for r in range(rows)
        for c in range(cols)
        if 0 <= r + down < rows and 0 <= c + right < cols
    ]
    return lax.ppermute(shard, ("row", "col"), pairs)


def local(scan, anchors, targets, *network):
    size = scan.shape[0]
    row_index = lax.axis_index("row")
    col_index = lax.axis_index("col")
    pixels = scan.astype(jnp.bfloat16)
    corners = anchors.reshape(-1, 2)
    live = (corners[:, 0] >= 0).astype(jnp.int32)
    here = jnp.stack([row_index, col_index]) * size
    own = jnp.concatenate(
        [live[:, None], corners - here[None], targets.reshape(-1, 1).astype(jnp.int32)], 1
    )
    ways = ((0, 1), (1, 0), (1, 1))
    reach = [own]
    for down, right in ways:
        info = moved(own, down, right)
        there = (row_index >= down) & (col_index >= right)
        shift = jnp.array([0, -down * size, -right * size, 0], jnp.int32)
        info = info + shift
        hit = there & (info[:, 0] != 0) & (info[:, 1] > -WIN) & (info[:, 2] > -WIN)
        reach.append(jnp.where(hit[:, None], info, 0))
    below = moved(pixels[:WIN], -1, 0)
    right = moved(pixels[:, :WIN], 0, -1)
    corner = moved(pixels[:WIN, :WIN], -1, -1)
    framed = jnp.concatenate(
        [jnp.concatenate([pixels, right], 1), jnp.concatenate([below, corner], 1)], 0
    )
    maps, scores = networks(framed, own, *network)
    maps = maps.astype(jnp.bfloat16)
    every = jnp.concatenate([maps] + [moved(maps, down, right) for down, right in ways], 0)
    saliency = blend(jnp.concatenate(reach, 0), every, size)
    return saliency, scores.reshape(targets.shape)


def solution(mesh):
    placed = (
        P("row", "col"),
        P(None, "row", "col", None),
        P(None, "row", "col"),
    ) + (P(),) * 8
    return jax.shard_map(
        local,
        mesh=mesh,
        in_specs=placed,
        out_specs=(P("row", "col"), P(None, "row", "col")),
        check_vma=False,
    )
```

time: 1470 us -> 264 us (0.18); the launches traced: 1440 us -> 262 us
  blocking collectives: 434 us -> 0 us
  matrix products: 376 us -> 1.08 us
  local copies, waits for them, and re-layouts: 277 us -> 15.2 us
  other arithmetic: 214 us -> 22.9 us
  Pallas kernels: 0 us -> 93.3 us
  starting transfers between devices: 16.6 us -> 104 us
  waiting for transfers between devices: 79.3 us -> 24.6 us
  loops' own time: 45.2 us -> 0 us
    all_gather x1 -> x0, blocking collectives: 434 us -> none  [local(): lax.all_gather(corners_flat, ('row', 'col'), axis=0, tiled=True)]
    conv_general_dilated x10 -> x0, matrix products: 359 us -> none  [convolve(): lax.conv_general_dilated(inputs[None], kernel, (stride, stride), ((margin...]
    conv_general_dilated x20 -> x0, local copies, waits for them, and re-layouts: 177 us -> none  [convolve(): lax.conv_general_dilated(inputs[None], kernel, (stride, stride), ((margin...]
    another operation x3 -> x1, other arithmetic: 148 us -> 0.01 us  [networks(): jnp.stack([stem_bias, conv1_bias, conv2_bias])[:, :, None]]
    pallas_call x0 -> x2, Pallas kernels: none -> 93.3 us  [the longest x1 83.7 us: networks(): pl.pallas_call(net_kernel, grid_spec=pltpu.PrefetchScalarGridSpec(num_sca...]
    ppermute x4 -> x9, starting transfers between devices: 16.6 us -> 104 us  [moved(): return lax.ppermute(shard, ('row', 'col'), pairs)]
    ppermute x4 -> x9, waiting for transfers between devices: 79.3 us -> 24.6 us  [moved(): return lax.ppermute(shard, ('row', 'col'), pairs)]
    another operation x6 -> x0, loops' own time: 45.2 us -> none  [the longest x1 18 us: run_windows(): return lax.fori_loop(0, crop_count, handle, (blank_contribs, blank_scores))]
  transfers between devices with their start and end apart: 4 -> 9, of which waited for: 3 -> 2; matrix products, arithmetic and copies ran while one was open for 0% -> 8% of each run, Pallas kernels for 0% -> 0%
where the time goes in v1:
time: 264 us; the launch traced here: 262 us
  starting transfers between devices  104 us (39%)
  Pallas kernels  93.3 us (35%)
  waiting for transfers between devices  24.6 us (9%)
  other arithmetic  22.9 us (9%)
  local copies, waits for them, and re-layouts  15.2 us (6%)
    ppermute x9, starting transfers between devices, moved(): return lax.ppermute(shard, ('row', 'col'), pairs)  104 us
    pallas_call x1, Pallas kernels, networks(): pl.pallas_call(net_kernel, grid_spec=pltpu.PrefetchScalarGridSpec(num_sca...  83.7 us
    ppermute x9, waiting for transfers between devices, moved(): return lax.ppermute(shard, ('row', 'col'), pairs)  24.6 us
    concatenate x1, other arithmetic, local(): jnp.concatenate([jnp.concatenate([pixels, right], 1), jnp.concatenate([be...  13.9 us
    pallas_call x1, Pallas kernels, blend(): pl.pallas_call(blend_kernel, grid_spec=pltpu.PrefetchScalarGridSpec(num_s...  9.59 us
  transfers between devices with their start and end apart: 9, of which 2 were waited for; matrix products, arithmetic and copies ran while one was open for 8% of the time, Pallas kernels for 0%

profile of v1, /device:TPU:36, one launch (start us, length us, event | category | flops | bytes accessed | tf_op | source)
XLA Modules:
  0.0 261.8 jit_solution(4376259813578005790)
XLA Ops:
  2.6 1.3 reduce.11
  4.1 3.4 %collective-permute-start.2 = (s32[4,4]{1,0:T(4,128)S(1)}, s32[4,4]{1,0:T(4,128)S(1)}, u32[]{:S(2)}, u32[]{:S(2)}) collective-permute-start(s32[4,4]{1,0:T(4,128)S(1)} %pad_add_fusion.1.info), channel_id=1, source_target_pairs={{0,33},{1,34},{2,35},{3,36},{4,37},{5,38},{6,39},{7,40},{8,41},{9,... | collective-permute-start | bytes 200 | tf_op jit(solution)/shard_map/ppermute | solution.py:314
  7.5 3.6 %collective-permute-start = (s32[4,4]{1,0:T(4,128)S(1)}, s32[4,4]{1,0:T(4,128)S(1)}, u32[]{:S(2)}, u32[]{:S(2)}) collective-permute-start(s32[4,4]{1,0:T(4,128)S(1)} %pad_add_fusion.1.info), channel_id=1, source_target_pairs={{0,1},{1,2},{2,3},{3,4},{4,5},{5,6},{6,7},{7,8},{8,9},{9,10},{10,1... | collective-permute-start | bytes 200 | tf_op jit(solution)/shard_map/ppermute | solution.py:314
  11.1 3.5 %collective-permute-start.1 = (s32[4,4]{1,0:T(4,128)S(1)}, s32[4,4]{1,0:T(4,128)S(1)}, u32[]{:S(2)}, u32[]{:S(2)}) collective-permute-start(s32[4,4]{1,0:T(4,128)S(1)} %pad_add_fusion.1.info), channel_id=1, source_target_pairs={{0,32},{1,33},{2,34},{3,35},{4,36},{5,37},{6,38},{7,39},{8,40},{9,... | collective-permute-start | bytes 200 | tf_op jit(solution)/shard_map/ppermute | solution.py:314
  14.6 2.5 convert_element_type.33
  17.2 1.1 slice.56
  18.2 3.8 %collective-permute-start.3 = (bf16[1024,512]{1,0:T(8,128)(2,1)}, bf16[1024,512]{1,0:T(8,128)(2,1)}, u32[]{:S(2)}, u32[]{:S(2)}) collective-permute-start(bf16[1024,512]{1,0:T(8,128)(2,1)} %slice.56), channel_id=1, source_target_pairs={{1,0},{2,1},{3,2},{4,3},{5,4},{6,5},{7,6},{8,7},{9,8},{10,9},{11,1... | collective-permute-start | bytes 3145736 | tf_op jit(solution)/shard_map/ppermute | solution.py:314
  22.0 1.0 slice.57
  23.1 2.3 collective-permute-start.4
  25.4 0.8 slice.58
  27.6 0.7 copy.64
  28.9 1.0 copy.70.stem_w
  29.9 0.9 convert_bitcast_fusion
  30.8 0.9 copy.68
  31.7 0.9 reverse_bitcast_fusion
  32.8 0.8 reshape.103.back_w
  33.6 1.1 copy.65
  34.6 0.8 reshape.101.first_w
  35.4 1.1 copy.66
  36.5 0.8 reshape.102.second_w
  38.6 1.9 collective-permute-start.5
  41.4 18.7 %collective-permute-done.5 = bf16[512,512]{1,0:T(8,128)(2,1)S(1)} collective-permute-done((bf16[512,512]{1,0:T(8,128)(2,1)}, bf16[512,512]{1,0:T(8,128)(2,1)S(1)}, u32[]{:S(2)}, u32[]{:S(2)}) %collective-permute-start.5) | collective-permute-done | bytes 524320 | tf_op jit(solution)/shard_map/ppermute | solution.py:314
  60.1 13.9 %maximum_maximum_fusion.source = bf16[1536,1536]{1,0:T(8,128)(2,1)} fusion(bf16[512,512]{1,0:T(8,128)(2,1)S(1)} %collective-permute-done.5, bf16[512,1024]{1,0:T(8,128)(2,1)} %collective-permute-done.4, bf16[1024,512]{1,0:T(8,128)(2,1)} %collective-permute-done.3, bf16[1024,1024]{1,0:T(8,128)(2,1)S(1)} %convert_element_type.33), kind=kLoop, calls=%fused_computation | loop fusion | flops 18874368 | bytes 9437184 | tf_op jit(solution)/shard_map/concatenate | solution.py:340
  74.0 0.7 broadcast_in_dim.60.biases
  74.7 83.7 %shard_map.149 = (f32[4,128,128]{2,1,0:T(8,128)}, f32[4,8,128]{2,1,0:T(8,128)}) custom-call(s32[4,4]{1,0:T(4,128)} %copy-done.1, bf16[1536,1536]{1,0:T(8,128)(2,1)} %maximum_maximum_fusion.source, bf16[1024,216]{1,0:T(8,128)(2,1)} %copy.70.stem_w, bf16[192,192]{1,0:T(8,128)(2,1)} %reshape.101.first_w, bf16[192,192]{1,0:T(8,128)(2,1)} %reshape.102.second_w, ...), custom_call_target="tpu_custom_call" | custom-call | tf_op jit(solution)/shard_map/pallas_call | solution.py:216
  158.4 1.0 convert_element_type.40
  159.4 2.1 collective-permute-start.6
  161.5 81.3 %collective-permute-start.7 = (bf16[4,128,128]{2,1,0:T(8,128)(2,1)S(1)}, bf16[4,128,128]{2,1,0:T(8,128)(2,1)S(1)}, u32[]{:S(2)}, u32[]{:S(2)}) collective-permute-start(bf16[4,128,128]{2,1,0:T(8,128)(2,1)S(1)} %convert_element_type.40), channel_id=1, source_target_pairs={{0,32},{1,33},{2,34},{3,35},{4,36},{5,37},{6,38},{7,39},{8,40},{9,... | collective-permute-start | bytes 393224 | tf_op jit(solution)/shard_map/ppermute | solution.py:314
  242.9 1.9 collective-permute-start.8
  244.9 0.8 slice_reduce_fusion
  246.3 5.8 %collective-permute-done.8 = bf16[4,128,128]{2,1,0:T(8,128)(2,1)S(1)} collective-permute-done((bf16[4,128,128]{2,1,0:T(8,128)(2,1)S(1)}, bf16[4,128,128]{2,1,0:T(8,128)(2,1)S(1)}, u32[]{:S(2)}, u32[]{:S(2)}) %collective-permute-start.8) | collective-permute-done | bytes 131104 | tf_op jit(solution)/shard_map/ppermute | solution.py:314
  252.2 9.6 %shard_map.150 = f32[1024,1024]{1,0:T(8,128)} custom-call(s32[16,4]{1,0:T(8,128)S(1)} %pad_add_fusion.info, bf16[16,128,128]{2,1,0:T(8,128)(2,1)S(1)} %pad_maximum_fusion.maps), custom_call_target="tpu_custom_call" | custom-call | tf_op jit(solution)/shard_map/pallas_call | solution.py:292
  (57 shorter events, 7.0 us)
Async XLA Ops:
  4.1 19.0 %copy-start.1 = (s32[4,4]{1,0:T(4,128)}, s32[4,4]{1,0:T(4,128)S(1)}, u32[]{:S(2)}) copy-start(s32[4,4]{1,0:T(4,128)S(1)} %pad_add_fusion.1.info) | copy-start | bytes 196
  4.1 22.3 %copy-start = (bf16[7,7,1,64]{3,1,2,0:T(8,128)(2,1)S(1)}, bf16[7,7,1,64]{3,1,2,0:T(8,128)(2,1)}, u32[]{:S(2)}) copy-start(bf16[7,7,1,64]{3,1,2,0:T(8,128)(2,1)} %param.17) | copy-start | bytes 18820
  4.1 34.5 %collective-permute-start.2 = (s32[4,4]{1,0:T(4,128)S(1)}, s32[4,4]{1,0:T(4,128)S(1)}, u32[]{:S(2)}, u32[]{:S(2)}) collective-permute-start(s32[4,4]{1,0:T(4,128)S(1)} %pad_add_fusion.1.info), channel_id=1, source_target_pairs={{0,33},{1,34},{2,35},{3,36},{4,37},{5,38},{6,39},{7,40},{8,41},{9,... | collective-permute-start | bytes 200 | tf_op jit(solution)/shard_map/ppermute | solution.py:314
  7.5 33.2 %collective-permute-start = (s32[4,4]{1,0:T(4,128)S(1)}, s32[4,4]{1,0:T(4,128)S(1)}, u32[]{:S(2)}, u32[]{:S(2)}) collective-permute-start(s32[4,4]{1,0:T(4,128)S(1)} %pad_add_fusion.1.info), channel_id=1, source_target_pairs={{0,1},{1,2},{2,3},{3,4},{4,5},{5,6},{6,7},{7,8},{8,9},{9,10},{10,1... | collective-permute-start | bytes 200 | tf_op jit(solution)/shard_map/ppermute | solution.py:314
  11.1 29.8 %collective-permute-start.1 = (s32[4,4]{1,0:T(4,128)S(1)}, s32[4,4]{1,0:T(4,128)S(1)}, u32[]{:S(2)}, u32[]{:S(2)}) collective-permute-start(s32[4,4]{1,0:T(4,128)S(1)} %pad_add_fusion.1.info), channel_id=1, source_target_pairs={{0,32},{1,33},{2,34},{3,35},{4,36},{5,37},{6,38},{7,39},{8,40},{9,... | collective-permute-start | bytes 200 | tf_op jit(solution)/shard_map/ppermute | solution.py:314
  18.2 41.9 %collective-permute-start.3 = (bf16[1024,512]{1,0:T(8,128)(2,1)}, bf16[1024,512]{1,0:T(8,128)(2,1)}, u32[]{:S(2)}, u32[]{:S(2)}) collective-permute-start(bf16[1024,512]{1,0:T(8,128)(2,1)} %slice.56), channel_id=1, source_target_pairs={{1,0},{2,1},{3,2},{4,3},{5,4},{6,5},{7,6},{8,7},{9,8},{10,9},{11,1... | collective-permute-start | bytes 3145736 | tf_op jit(solution)/shard_map/ppermute | solution.py:314
  23.1 37.0 %collective-permute-start.4 = (bf16[512,1024]{1,0:T(8,128)(2,1)}, bf16[512,1024]{1,0:T(8,128)(2,1)}, u32[]{:S(2)}, u32[]{:S(2)}) collective-permute-start(bf16[512,1024]{1,0:T(8,128)(2,1)} %slice.57), channel_id=1, source_target_pairs={{32,0},{33,1},{34,2},{35,3},{36,4},{37,5},{38,6},{39,7},{40,8},{41... | collective-permute-start | bytes 3145736 | tf_op jit(solution)/shard_map/ppermute | solution.py:314
  26.8 10.5 %copy-start.2 = (bf16[64,9]{0,1:T(8,128)(2,1)S(1)}, bf16[64,9]{0,1:T(8,128)(2,1)}, u32[]{:S(2)}) copy-start(bf16[64,9]{0,1:T(8,128)(2,1)} %param.23) | copy-start | bytes 3460
  26.8 11.2 %copy-start.6 = (f32[64]{0:T(128)S(1)}, f32[64]{0:T(128)}, u32[]{:S(2)}) copy-start(f32[64]{0:T(128)} %param.22) | copy-start | bytes 772
  26.8 11.2 %copy-start.7 = (f32[64]{0:T(128)S(1)}, f32[64]{0:T(128)}, u32[]{:S(2)}) copy-start(f32[64]{0:T(128)} %param.20) | copy-start | bytes 772
  26.8 11.2 %copy-start.8 = (f32[64]{0:T(128)S(1)}, f32[64]{0:T(128)}, u32[]{:S(2)}) copy-start(f32[64]{0:T(128)} %param.18) | copy-start | bytes 772
  26.8 11.2 %copy-start.9 = (f32[9]{0:T(128)S(1)}, f32[9]{0:T(128)}, u32[]{:S(2)}) copy-start(f32[9]{0:T(128)} %param.24) | copy-start | bytes 112
  26.8 13.6 %copy-start.5 = (s32[4]{0:T(128)S(1)}, s32[4]{0:T(128)}, u32[]{:S(2)}) copy-start(s32[4]{0:T(128)} %constant.33.clone) | copy-start | bytes 52
  26.9 13.9 %copy-start.4 = (s32[4]{0:T(128)S(1)}, s32[4]{0:T(128)}, u32[]{:S(2)}) copy-start(s32[4]{0:T(128)} %constant.31.clone) | copy-start | bytes 52
  26.9 14.1 %copy-start.3 = (s32[4]{0:T(128)S(1)}, s32[4]{0:T(128)}, u32[]{:S(2)}) copy-start(s32[4]{0:T(128)} %constant.32.clone) | copy-start | bytes 52
  38.6 21.5 %collective-permute-start.5 = (bf16[512,512]{1,0:T(8,128)(2,1)}, bf16[512,512]{1,0:T(8,128)(2,1)S(1)}, u32[]{:S(2)}, u32[]{:S(2)}) collective-permute-start(bf16[512,512]{1,0:T(8,128)(2,1)} %slice.58), channel_id=1, source_target_pairs={{33,0},{34,1},{35,2},{36,3},{37,4},{38,5},{39,6},{40,7},{41,8},{42... | collective-permute-start | bytes 1572872 | tf_op jit(solution)/shard_map/ppermute | solution.py:314
  159.4 86.9 %collective-permute-start.6 = (bf16[4,128,128]{2,1,0:T(8,128)(2,1)S(1)}, bf16[4,128,128]{2,1,0:T(8,128)(2,1)S(1)}, u32[]{:S(2)}, u32[]{:S(2)}) collective-permute-start(bf16[4,128,128]{2,1,0:T(8,128)(2,1)S(1)} %convert_element_type.40), channel_id=1, source_target_pairs={{0,1},{1,2},{2,3},{3,4},{4,5},{5,6},{6,7},{7,8},{8,9},{9,10},{10,1... | collective-permute-start | bytes 393224 | tf_op jit(solution)/shard_map/ppermute | solution.py:314
  161.5 84.8 %collective-permute-start.7 = (bf16[4,128,128]{2,1,0:T(8,128)(2,1)S(1)}, bf16[4,128,128]{2,1,0:T(8,128)(2,1)S(1)}, u32[]{:S(2)}, u32[]{:S(2)}) collective-permute-start(bf16[4,128,128]{2,1,0:T(8,128)(2,1)S(1)} %convert_element_type.40), channel_id=1, source_target_pairs={{0,32},{1,33},{2,34},{3,35},{4,36},{5,37},{6,38},{7,39},{8,40},{9,... | collective-permute-start | bytes 393224 | tf_op jit(solution)/shard_map/ppermute | solution.py:314
  242.9 9.3 %collective-permute-start.8 = (bf16[4,128,128]{2,1,0:T(8,128)(2,1)S(1)}, bf16[4,128,128]{2,1,0:T(8,128)(2,1)S(1)}, u32[]{:S(2)}, u32[]{:S(2)}) collective-permute-start(bf16[4,128,128]{2,1,0:T(8,128)(2,1)S(1)} %convert_element_type.40), channel_id=1, source_target_pairs={{0,33},{1,34},{2,35},{3,36},{4,37},{5,38},{6,39},{7,40},{8,41},{9,... | collective-permute-start | bytes 393224 | tf_op jit(solution)/shard_map/ppermute | solution.py:314

commit v2 on v1

v2 whole, which is shorter than its diff:
```python
import jax
import jax.numpy as jnp
from jax import lax
from jax.experimental import pallas as pl
from jax.experimental.pallas import tpu as pltpu
from jax.sharding import PartitionSpec as P

TILE = 1024
WIN = 512
RIM = 512
C = 64
F = 128
SLOTS = 4
BLOCKS = 16
ROWS = 64
LOW = -3.0e38
MESH = pl.DeviceIdType.MESH
WAYS = ((0, 0), (0, 1), (1, 0), (1, 1))


def lanes(shape):
    return lax.broadcasted_iota(jnp.int32, shape, len(shape) - 1)


def frame_kernel(
    scan, own, framed, infos,
    raw, pixels, loads, keeps, up_send, up_recv, left_send, left_recv,
    corner_send, corner_recv, info_send, info_recv,
):
    row, col = lax.axis_index("row"), lax.axis_index("col")
    rows, cols = lax.axis_size("row"), lax.axis_size("col")
    up, down, left, right = row > 0, row < rows - 1, col > 0, col < cols - 1
    chunks = TILE // F
    fetch = [
        pltpu.make_async_copy(scan.at[pl.ds(k * F, F)], raw.at[pl.ds(k * F, F)], loads.at[k])
        for k in range(chunks)
    ]
    for copy in fetch:
        copy.start()
    infos[...] = jnp.full_like(infos, -1)
    infos[0] = own[...]

    barrier = pltpu.get_barrier_semaphore()
    partners = (
        (-1, 0, up), (1, 0, down), (0, -1, left), (0, 1, right),
        (1, 1, down & right), (-1, -1, up & left),
    )
    for by_row, by_col, there in partners:
        @pl.when(there)
        def _():
            pl.semaphore_signal(
                barrier, inc=1, device_id=(row + by_row, col + by_col), device_id_type=MESH
            )
    pl.semaphore_wait(barrier, sum(there.astype(jnp.int32) for _, _, there in partners))

    def remote(source, target, send, recv, by_row, by_col):
        return pltpu.make_async_remote_copy(
            src_ref=source, dst_ref=target, send_sem=send, recv_sem=recv,
            device_id=(row + by_row, col + by_col), device_id_type=MESH,
        )

    def part(k):
        return pl.ds(k * F, F)

    def under(k):
        return pl.ds(TILE + k * F, F)

    ups = [
        remote(pixels.at[part(k)], framed.at[under(k), pl.ds(0, TILE)],
               up_send.at[k], up_recv.at[k], -1, 0)
        for k in range(RIM // F)
    ]
    lefts = [
        remote(pixels.at[part(k), pl.ds(0, RIM)], framed.at[part(k), pl.ds(TILE, RIM)],
               left_send.at[k], left_recv.at[k], 0, -1)
        for k in range(chunks)
    ]
    corners = [
        remote(framed.at[under(k), pl.ds(0, RIM)], framed.at[under(k), pl.ds(TILE, RIM)],
               corner_send.at[k], corner_recv.at[k], 0, -1)
        for k in range(RIM // F)
    ]
    tells = [
        (remote(own, infos.at[1], info_send.at[0], info_recv.at[0], 0, 1), right, left),
        (remote(own, infos.at[2], info_send.at[1], info_recv.at[1], 1, 0), down, up),
        (remote(own, infos.at[3], info_send.at[2], info_recv.at[2], 1, 1), down & right, up & left),
    ]
    kept = [
        pltpu.make_async_copy(pixels.at[part(k)], framed.at[part(k), pl.ds(0, TILE)], keeps.at[k])
        for k in range(chunks)
    ]
    for k in range(chunks):
        fetch[k].wait()
        pixels[k * F : (k + 1) * F, :] = raw[k * F : (k + 1) * F, :].astype(jnp.bfloat16)
        if k < len(ups):
            pl.when(up)(ups[k].start)
        pl.when(left)(lefts[k].start)
        kept[k].start()
    for tell, goes, _ in tells:
        pl.when(goes)(tell.start)
    for k in range(len(ups)):
        pl.when(down)(ups[k].wait_recv)
        pl.when(down & left)(corners[k].start)
    for tell, goes, comes in tells:
        pl.when(goes)(tell.wait_send)
        pl.when(comes)(tell.wait_recv)
    for k in range(chunks):
        kept[k].wait()
        pl.when(left)(lefts[k].wait_send)
        pl.when(right)(lefts[k].wait_recv)
        if k < len(ups):
            pl.when(up)(ups[k].wait_send)
            pl.when(down & left)(corners[k].wait_send)
            pl.when(down & right)(corners[k].wait_recv)


def frame(scan, own):
    chunks, rim = TILE // F, RIM // F
    sems = [chunks, chunks, rim, rim, chunks, chunks, rim, rim, 3, 3]
    return pl.pallas_call(
        frame_kernel,
        out_shape=[
            jax.ShapeDtypeStruct((TILE + RIM, TILE + RIM), jnp.bfloat16),
            jax.ShapeDtypeStruct((4, 8, F), jnp.int32),
        ],
        in_specs=[pl.BlockSpec(memory_space=pl.ANY), pl.BlockSpec(memory_space=pltpu.VMEM)],
        out_specs=[pl.BlockSpec(memory_space=pl.ANY), pl.BlockSpec(memory_space=pltpu.VMEM)],
        scratch_shapes=[
            pltpu.VMEM((TILE, TILE), jnp.float32),
            pltpu.VMEM((TILE, TILE), jnp.bfloat16),
        ] + [pltpu.SemaphoreType.DMA((n,)) for n in sems],
        compiler_params=pltpu.CompilerParams(
            collective_id=0, has_side_effects=True, vmem_limit_bytes=16 << 20
        ),
    )(scan, own)


def put_taps(ref, row, value):
    value = value.astype(jnp.bfloat16)
    lane = lanes((C, F))
    none = jnp.zeros((), jnp.bfloat16)
    ref[row, 0:C, :] = jnp.where(lane == 0, none, pltpu.roll(value, 1, 1))
    ref[row, C : 2 * C, :] = value
    ref[row, 2 * C : 3 * C, :] = jnp.where(lane == F - 1, none, pltpu.roll(value, F - 1, 1))


def convolved(taps_ref, weight_ref, finish):
    weight = weight_ref[...]
    zero = jnp.zeros((C, F), jnp.float32)

    def several(step, carried):
        near, far = carried
        base = step * ROWS
        data = jnp.concatenate([taps_ref[base + k] for k in range(ROWS)], 1)
        out = jnp.dot(weight, data, preferred_element_type=jnp.float32)
        part = lambda tap, k: out[tap * C : (tap + 1) * C, k * F : (k + 1) * F]
        finish(base - 1, near + part(2, 0))
        finish(base, far + part(1, 0) + part(2, 1))
        for k in range(1, ROWS - 1):
            finish(base + k, part(0, k - 1) + part(1, k) + part(2, k + 1))
        return part(0, ROWS - 2) + part(1, ROWS - 1), part(0, ROWS - 1)

    near, _ = lax.fori_loop(0, F // ROWS, several, (zero, zero))
    finish(F - 1, near)


def arrange(stem_raw, first_raw, second_raw, biases_raw, stem_w, first_w, second_w, back_w, biases):
    turned = stem_raw[...].astype(jnp.float32).T.astype(jnp.bfloat16)
    tap = lax.broadcasted_iota(jnp.int32, (49, 216), 0)
    tap_row, tap_col = tap // 7, tap % 7
    place_col, place_row = lanes((49, 216)) // 24, lanes((49, 216)) % 24
    for r in range(8):
        for q in range(2):
            hit = (place_row == 2 * r + tap_row) & (place_col == 2 * q + tap_col)
            hit = jnp.where(hit, 1.0, 0.0).astype(jnp.bfloat16)
            at = (r * 2 + q) * C
            stem_w[at : at + C, :] = jnp.dot(
                turned, hit, preferred_element_type=jnp.float32
            ).astype(jnp.bfloat16)
    for raw, laid in ((first_raw, first_w), (second_raw, second_w)):
        for dy in range(3):
            block = raw[dy * 3 : dy * 3 + 3].reshape(3 * C, C).astype(jnp.float32)
            laid[dy * C : (dy + 1) * C, :] = block.T.astype(jnp.bfloat16)
    for dy in range(3):
        blocks = [second_raw[(2 - dy) * 3 + (2 - dx)] for dx in range(3)]
        back_w[dy * C : (dy + 1) * C, :] = jnp.concatenate(blocks, 1)
    eye = lax.broadcasted_iota(jnp.int32, (C, C), 0) == lanes((C, C))
    for k in range(3):
        upright = jnp.sum(jnp.where(eye, biases_raw[k : k + 1, :], 0.0), 1, keepdims=True)
        biases[k] = jnp.broadcast_to(upright, (C, F))


def net_kernel(
    infos, source, stem_raw, first_raw, second_raw, biases_raw, heads, head_bias,
    map_ref, logit_ref,
    stem_w, first_w, second_w, back_w, biases,
    pixels, spread_ref, picked, feats, hidden, grads, acc, order, arrival,
):
    count = jnp.int32(0)
    for slot in range(SLOTS):
        live = infos[0, slot, 0] >= 0

        @pl.when(live)
        def _():
            order[count] = slot

        count = count + live.astype(jnp.int32)

    def place(number):
        slot = order[number]
        return slot, infos[0, slot, 0] % TILE, infos[0, slot, 1] % TILE, infos[0, slot, 2]

    def fetch(number):
        _, top, left, _ = place(number)
        row0 = pl.multiple_of(top // 16 * 16, 16)
        col0 = pl.multiple_of(left // F * F, F)
        here = number % 2
        return pltpu.make_async_copy(
            source.at[pl.ds(row0, 528), pl.ds(col0, 640)], pixels.at[here], arrival.at[here]
        )

    @pl.when(count > 0)
    def _():
        fetch(0).start()

    arrange(
        stem_raw, first_raw, second_raw, biases_raw, stem_w, first_w, second_w, back_w, biases
    )
    map_ref[...] = jnp.zeros_like(map_ref)
    logit_ref[...] = jnp.zeros_like(logit_ref)

    def window(number, _):
        slot, top, left, target = place(number)

        @pl.when(number + 1 < count)
        def _():
            fetch(number + 1).start()

        over = left % F
        for u in range(9):
            at = lax.broadcasted_iota(jnp.int32, (640, F), 0) - over
            want = lanes((640, F)) * 4 + (u - 3)
            hit = (at == want) & (want >= 0) & (want < WIN)
            spread_ref[:, u * F : (u + 1) * F] = jnp.where(hit, 1.0, 0.0).astype(jnp.bfloat16)
        below = top % 16
        row = lax.broadcasted_iota(jnp.int32, (520, 528), 0) - 3
        shift = jnp.where(
            (lanes((520, 528)) - below == row) & (row >= 0) & (row < WIN), 1.0, 0.0
        ).astype(jnp.bfloat16)
        fetch(number).wait()
        row = lax.broadcasted_iota(jnp.int32, (528, 640), 0) - below
        column = lanes((528, 640)) - over
        inside = (row >= 0) & (row < WIN) & (column >= 0) & (column < WIN)
        found = jnp.where(inside, pixels[number % 2].astype(jnp.float32), 0.0)
        moved = jnp.dot(shift, found.astype(jnp.bfloat16), preferred_element_type=jnp.float32)
        picked[...] = jnp.dot(
            moved.astype(jnp.bfloat16), spread_ref[...], preferred_element_type=jnp.float32
        )
        stem_bias = biases[0]
        lane0 = lanes((C, F)) == 0
        none = jnp.zeros((), jnp.bfloat16)

        def stem(step, carried):
            even, odd = carried
            slabs = []
            for k in range(BLOCKS):
                start = pl.multiple_of((step * BLOCKS + k) * 16, 16)
                slab = [picked[pl.ds(start, 24), u * F : (u + 1) * F] for u in range(9)]
                slabs.append(jnp.concatenate(slab, 0))
            data = jnp.concatenate(slabs, 1).astype(jnp.bfloat16)
            out = jnp.dot(stem_w[...], data, preferred_element_type=jnp.float32)
            for k in range(BLOCKS):
                for r in range(4):
                    part = lambda n: out[
                        (r * 4 + n) * C : (r * 4 + n + 1) * C, k * F : (k + 1) * F
                    ]
                    e_high = jnp.maximum(jnp.maximum(even, part(0)), part(2))
                    o_high = jnp.maximum(jnp.maximum(odd, part(1)), part(3))
                    even, odd = part(2), part(3)
                    high = jnp.maximum(e_high, o_high) + stem_bias
                    high = jnp.maximum(high, 0.0).astype(jnp.bfloat16)
                    side = jnp.maximum(o_high + stem_bias, 0.0).astype(jnp.bfloat16)
                    before = jnp.where(lane0, none, pltpu.roll(side, 1, 1))
                    put_taps(feats, (step * BLOCKS + k) * 4 + r, jnp.maximum(high, before))
            return even, odd

        low = jnp.full((C, F), LOW, jnp.float32)
        lax.fori_loop(0, F // 4 // BLOCKS, stem, (low, low))

        def after_first(row, sums):
            put_taps(hidden, jnp.maximum(row, 0), jnp.maximum(sums + biases[1], 0.0))

        convolved(feats, first_w, after_first)

        head = jnp.where(lanes((C, 9)) == target, heads[...].astype(jnp.float32), 0.0)
        column = jnp.sum(head, 1, keepdims=True)
        grad = jnp.broadcast_to(
            (column / float(F * F)).astype(jnp.bfloat16).astype(jnp.float32), (C, F)
        )
        acc[...] = jnp.zeros_like(acc)

        def after_second(row, sums):
            keep = jnp.where(row >= 0, 1.0, 0.0)
            row = jnp.maximum(row, 0)
            value = sums + feats[row, C : 2 * C, :].astype(jnp.float32) + biases[2]
            value = jnp.maximum(value, 0.0)
            out = jnp.where(value > 0, grad, 0.0)
            acc[0] += value * keep
            acc[1] += out * keep
            put_taps(grads, row, out)

        convolved(hidden, second_w, after_second)

        def after_back(row, sums):
            keep = jnp.where(row >= 0, 1.0, 0.0)
            row = jnp.maximum(row, 0)
            open_ = hidden[row, C : 2 * C, :].astype(jnp.float32) > 0
            value = jnp.where(open_, sums, 0.0).astype(jnp.bfloat16).astype(jnp.float32)
            acc[2] += value * keep
            acc[3] = jnp.where(row == 0, value, acc[3])
            acc[4] = value

        convolved(grads, back_w, after_back)

        mean = jnp.sum(acc[0], 1, keepdims=True) / float(F * F)
        logit = jnp.sum(mean * column)
        bias = jnp.sum(jnp.where(lanes((1, 9)) == target, head_bias[...], 0.0))
        logit_ref[slot] = jnp.full((8, F), logit + bias, jnp.float32)

        whole = acc[2]
        parts = [whole - acc[4], whole, whole - acc[3]]
        lane = lanes((C, F))
        eye = lax.broadcasted_iota(jnp.int32, (C, C), 0) == lanes((C, C))
        channel = jnp.sum(acc[1], 1, keepdims=True)
        for dy in range(3):
            for dx in range(3):
                drop = {0: F - 1, 1: F, 2: 0}[dx]
                total = jnp.sum(jnp.where(lane == drop, 0.0, parts[dy]), 1, keepdims=True)
                flat = jnp.sum(jnp.where(eye, total, 0.0), 0, keepdims=True)
                weight = first_raw[(2 - dy) * 3 + (2 - dx)].astype(jnp.float32)
                channel = channel + jnp.sum(weight * flat, 1, keepdims=True)
        channel = jnp.broadcast_to(channel, (C, F))

        def rows(step, _):
            base = pl.multiple_of(step * 16, 16)
            found = [
                jnp.sum(
                    feats[base + k, C : 2 * C, :].astype(jnp.float32) * channel, 0, keepdims=True
                )
                for k in range(16)
            ]
            found = jnp.maximum(jnp.concatenate(found, 0), 0.0)
            map_ref[slot, pl.ds(base, 16), :] = found.astype(jnp.bfloat16)
            return 0

        lax.fori_loop(0, F // 16, rows, 0)
        return 0

    lax.fori_loop(0, count, window, 0)


def networks(infos, framed, stem_weight, stem_bias, conv1_weight, conv1_bias, conv2_weight,
             conv2_bias, head_weight, head_bias):
    biases = jnp.stack([stem_bias, conv1_bias, conv2_bias])
    whole = pl.BlockSpec(memory_space=pltpu.VMEM)
    maps, logits = pl.pallas_call(
        net_kernel,
        in_specs=[pl.BlockSpec(memory_space=pltpu.SMEM), pl.BlockSpec(memory_space=pl.ANY)]
        + [whole] * 6,
        out_specs=[whole, whole],
        scratch_shapes=[
            pltpu.VMEM((16 * C, 216), jnp.bfloat16),
            pltpu.VMEM((3 * C, 3 * C), jnp.bfloat16),
            pltpu.VMEM((3 * C, 3 * C), jnp.bfloat16),
            pltpu.VMEM((3 * C, 3 * C), jnp.bfloat16),
            pltpu.VMEM((3, C, F), jnp.float32),
            pltpu.VMEM((2, 528, 640), jnp.bfloat16),
            pltpu.VMEM((640, 9 * F), jnp.bfloat16),
            pltpu.VMEM((520, 9 * F), jnp.float32),
            pltpu.VMEM((F, 3 * C, F), jnp.bfloat16),
            pltpu.VMEM((F, 3 * C, F), jnp.bfloat16),
            pltpu.VMEM((F, 3 * C, F), jnp.bfloat16),
            pltpu.VMEM((5, C, F), jnp.float32),
            pltpu.SMEM((SLOTS,), jnp.int32),
            pltpu.SemaphoreType.DMA((2,)),
        ],
        out_shape=[
            jax.ShapeDtypeStruct((SLOTS, F, F), jnp.bfloat16),
            jax.ShapeDtypeStruct((SLOTS, 8, F), jnp.float32),
        ],
        compiler_params=pltpu.CompilerParams(vmem_limit_bytes=58 << 20),
    )(
        infos, framed, stem_weight.reshape(49, C), conv1_weight.reshape(9, C, C),
        conv2_weight.reshape(9, C, C), biases, head_weight, head_bias.reshape(1, 9),
    )
    return maps, logits[:, 0, 0]


def blend_kernel(infos, maps, out_ref, total):
    out_ref[...] = jnp.zeros_like(out_ref)
    total[...] = jnp.zeros_like(total)

    def profile(offset):
        value = (offset - (WIN - 1) / 2.0) * (1.0 / (WIN / 4.0))
        return jnp.exp(-0.5 * value * value)

    def window(number, _):
        way, slot = number // SLOTS, number % SLOTS
        corner = infos[way, slot, 0]
        top = corner % TILE - way // 2 * TILE
        left = infos[way, slot, 1] % TILE - way % 2 * TILE

        @pl.when((corner >= 0) & (top > -WIN) & (left > -WIN))
        def _():
            row0 = pl.multiple_of(jnp.clip(top // 8 * 8, 0, TILE - 520), 8)
            col0 = pl.multiple_of(jnp.clip(left // F * F, 0, TILE - 640), F)
            row = lax.broadcasted_iota(jnp.int32, (520, F), 0) + (row0 - top)
            in_row = (row >= 0) & (row < WIN)
            up = jnp.where(in_row & (row // 4 == lanes((520, F))), 1.0, 0.0)
            down = jnp.where(in_row, profile(row.astype(jnp.float32)), 0.0)
            col = lanes((F, 640)) + (col0 - left)
            in_col = (col >= 0) & (col < WIN)
            tap = lax.broadcasted_iota(jnp.int32, (F, 640), 0)
            across = jnp.where(in_col & (col // 4 == tap), 1.0, 0.0).astype(jnp.bfloat16)
            col = lanes((8, 640)) + (col0 - left)
            in_col = (col >= 0) & (col < WIN)
            side = jnp.where(in_col, profile(col.astype(jnp.float32)), 0.0)[0:1]
            tall = jnp.dot(
                up.astype(jnp.bfloat16), maps[number], preferred_element_type=jnp.float32
            ).astype(jnp.bfloat16)
            for k in range(5):
                part = slice(k * F, (k + 1) * F)
                at = (pl.ds(row0, 520), pl.ds(pl.multiple_of(col0 + k * F, F), F))
                weight = down * side[:, part]
                value = jnp.dot(tall, across[:, part], preferred_element_type=jnp.float32)
                out_ref[at] += value * weight
                total[at] += weight
        return 0

    lax.fori_loop(0, 4 * SLOTS, window, 0)
    out_ref[...] = out_ref[...] / jnp.maximum(total[...], 1.0)


def blend(infos, maps):
    return pl.pallas_call(
        blend_kernel,
        in_specs=[
            pl.BlockSpec(memory_space=pltpu.SMEM),
            pl.BlockSpec(memory_space=pltpu.VMEM),
        ],
        out_specs=pl.BlockSpec(memory_space=pltpu.VMEM),
        scratch_shapes=[pltpu.VMEM((TILE, TILE), jnp.float32)],
        out_shape=jax.ShapeDtypeStruct((TILE, TILE), jnp.float32),
        compiler_params=pltpu.CompilerParams(vmem_limit_bytes=40 << 20),
    )(infos, maps)


def moved(shard, down, right):
    rows, cols = lax.axis_size("row"), lax.axis_size("col")
    pairs = [
        (r * cols + c, (r + down) * cols + c + right)
        for r in range(rows)
        for c in range(cols)
        if 0 <= r + down < rows and 0 <= c + right < cols
    ]
    return lax.ppermute(shard, ("row", "col"), pairs)


def local(scan, anchors, targets, *network):
    own = jnp.concatenate([anchors.reshape(SLOTS, 2), targets.reshape(SLOTS, 1)], 1)
    own = jnp.pad(own, ((0, 8 - SLOTS), (0, F - 3)), constant_values=-1)
    framed, infos = frame(scan, own)
    maps, scores = networks(infos, framed, *network)
    every = jnp.concatenate([maps] + [moved(maps, *way) for way in WAYS[1:]], 0)
    saliency = blend(infos, every)
    return saliency, scores.reshape(targets.shape)


def solution(mesh):
    placed = (
        P("row", "col"),
        P(None, "row", "col", None),
        P(None, "row", "col"),
    ) + (P(),) * 8
    return jax.shard_map(
        local,
        mesh=mesh,
        in_specs=placed,
        out_specs=(P("row", "col"), P(None, "row", "col")),
        check_vma=False,
    )
```

time: 264 us -> 118 us (0.45)
  the two profiles are of different devices: /device:TPU:36 before, /device:TPU:70 now
where the time goes in v2:
time: 118 us; the launch traced here: 117 us
  Pallas kernels  92 us (78%)
  local copies, waits for them, and re-layouts  9.71 us (8%)
  starting transfers between devices  5.76 us (5%)
  waiting for transfers between devices  5.2 us (4%)
  other arithmetic  3.66 us (3%)
    pallas_call x1, Pallas kernels, networks(): pl.pallas_call(net_kernel, in_specs=[pl.BlockSpec(memory_space=pltpu.SMEM...  49.8 us
    pallas_call x1, Pallas kernels, frame(): pl.pallas_call(frame_kernel, out_shape=[jax.ShapeDtypeStruct((TILE + RIM,...  30 us
    pallas_call x1, Pallas kernels, blend(): pl.pallas_call(blend_kernel, in_specs=[pl.BlockSpec(memory_space=pltpu.SM...  12.2 us
    unnamed x16, local copies, waits for them, and re-layouts  6.82 us
    ppermute x3, starting transfers between devices, moved(): return lax.ppermute(shard, ('row', 'col'), pairs)  5.76 us
    ppermute x3, waiting for transfers between devices, moved(): return lax.ppermute(shard, ('row', 'col'), pairs)  5.2 us
  transfers between devices with their start and end apart: 3, of which 3 were waited for; matrix products, arithmetic and copies ran while one was open for 1% of the time, Pallas kernels for 0%

profile of v2, /device:TPU:70, one launch (start us, length us, event | category | flops | bytes accessed | tf_op | source)
XLA Modules:
  0.0 117.1 jit_solution(17410078259289084089)
XLA Ops:
  0.6 0.0 copy-start.4
  0.6 0.0 copy-start.5
  0.7 0.0 copy-start.6
  0.7 0.5 broadcast.6
  1.2 1.3 %reduce.5 = s32[2,2]{1,0:T(2,128)S(1)} reduce(s32[2,2,1]{1,2,0:T(1,128)} %param.13, s32[]{:T(128)} %broadcast.6), dimensions={2}, to_apply=%param.13.reduce_sub_computation.3 | reduce | bytes 36 | tf_op args[2]
  2.5 0.1 reshape.28
  2.6 1.3 %reshape.24.stem_raw = bf16[49,64]{1,0:T(8,128)(2,1)} reshape(bf16[7,7,1,64]{3,1,2,0:T(8,128)(2,1)} %param.14) | data formatting | bytes 12544 | tf_op jit(solution)/shard_map/reshape | solution.py:393
  3.9 1.4 %copy.21.heads = bf16[64,9]{1,0:T(8,128)(2,1)} copy(bf16[64,9]{0,1:T(8,128)(2,1)} %param.20) | data formatting | bytes 2304 | tf_op args[9]
  5.3 0.8 pad_add_fusion
  6.1 0.0 copy-start.1
  6.1 2.2 %copy-done.1 = f32[1024,1024]{1,0:T(8,128)S(1)} copy-done((f32[1024,1024]{1,0:T(8,128)S(1)}, f32[1024,1024]{1,0:T(8,128)}, u32[]{:S(2)}) %copy-start.1) | copy-done | bytes 4194328
  8.3 30.0 %shard_map.122 = (bf16[1536,1536]{1,0:T(8,128)(2,1)S(1)}, s32[4,8,128]{2,1,0:T(8,128)S(1)}) custom-call(f32[1024,1024]{1,0:T(8,128)S(1)} %copy-done.1, s32[8,128]{1,0:T(8,128)S(1)} %pad.4.own), custom_call_target="tpu_custom_call" | custom-call | tf_op jit(solution)/shard_map/pallas_call | solution.py:120
  38.3 0.0 copy-start
  38.3 2.1 %copy-done = bf16[1536,1536]{1,0:T(8,128)(2,1)} copy-done((bf16[1536,1536]{1,0:T(8,128)(2,1)}, bf16[1536,1536]{1,0:T(8,128)(2,1)S(1)}, u32[]{:S(2)}) %copy-start) | copy-done | bytes 4718616
  40.4 0.0 copy-start.2
  40.4 0.6 copy-done.2
  41.0 0.0 copy-done.4
  41.0 0.0 copy-done.5
  41.0 0.0 copy-done.6
  41.0 0.6 pad_maximum_fusion.1.biases_raw
  41.6 49.8 %shard_map.123 = (bf16[4,128,128]{2,1,0:T(8,128)(2,1)}, f32[4,8,128]{2,1,0:T(8,128)}) custom-call(s32[4,8,128]{2,1,0:T(8,128)} %copy-done.2, bf16[1536,1536]{1,0:T(8,128)(2,1)} %copy-done, bf16[49,64]{1,0:T(8,128)(2,1)} %reshape.24.stem_raw, bf16[9,64,64]{2,1,0:T(8,128)(2,1)} %bitcast.11, bf16[9,64,64]{2,1,0:T(8,128)(2,1)} %bitcast.12, ...), custom_call_target="tpu_custom_call" | custom-call | tf_op jit(solution)/shard_map/pallas_call | solution.py:366
  91.4 1.9 %collective-permute-start.2 = (bf16[4,128,128]{2,1,0:T(8,128)(2,1)}, bf16[4,128,128]{2,1,0:T(8,128)(2,1)S(1)}, u32[]{:S(2)}, u32[]{:S(2)}) collective-permute-start(bf16[4,128,128]{2,1,0:T(8,128)(2,1)} %get-tuple-element.8), channel_id=1, source_target_pairs={{0,33},{1,34},{2,35},{3,36},{4,37},{5,38},{6,39},{7,40},{8,41},{9,... | collective-permute-start | bytes 393224 | tf_op jit(solution)/shard_map/ppermute | solution.py:466
  93.4 1.9 %collective-permute-start.1 = (bf16[4,128,128]{2,1,0:T(8,128)(2,1)}, bf16[4,128,128]{2,1,0:T(8,128)(2,1)S(1)}, u32[]{:S(2)}, u32[]{:S(2)}) collective-permute-start(bf16[4,128,128]{2,1,0:T(8,128)(2,1)} %get-tuple-element.8), channel_id=1, source_target_pairs={{0,32},{1,33},{2,34},{3,35},{4,36},{5,37},{6,38},{7,39},{8,40},{9,... | collective-permute-start | bytes 393224 | tf_op jit(solution)/shard_map/ppermute | solution.py:466
  95.3 1.9 %collective-permute-start = (bf16[4,128,128]{2,1,0:T(8,128)(2,1)}, bf16[4,128,128]{2,1,0:T(8,128)(2,1)S(1)}, u32[]{:S(2)}, u32[]{:S(2)}) collective-permute-start(bf16[4,128,128]{2,1,0:T(8,128)(2,1)} %get-tuple-element.8), channel_id=1, source_target_pairs={{0,1},{1,2},{2,3},{3,4},{4,5},{5,6},{6,7},{7,8},{8,9},{9,10},{10,1... | collective-permute-start | bytes 393224 | tf_op jit(solution)/shard_map/ppermute | solution.py:466
  97.2 0.8 slice_reduce_fusion
  98.1 0.6 reshape_squeeze.3
  98.7 2.4 %collective-permute-done.2 = bf16[4,128,128]{2,1,0:T(8,128)(2,1)S(1)} collective-permute-done((bf16[4,128,128]{2,1,0:T(8,128)(2,1)}, bf16[4,128,128]{2,1,0:T(8,128)(2,1)S(1)}, u32[]{:S(2)}, u32[]{:S(2)}) %collective-permute-start.2) | collective-permute-done | bytes 131104 | tf_op jit(solution)/shard_map/ppermute | solution.py:466
  101.1 0.8 collective-permute-done.1
  101.8 2.1 %collective-permute-done = bf16[4,128,128]{2,1,0:T(8,128)(2,1)S(1)} collective-permute-done((bf16[4,128,128]{2,1,0:T(8,128)(2,1)}, bf16[4,128,128]{2,1,0:T(8,128)(2,1)S(1)}, u32[]{:S(2)}, u32[]{:S(2)}) %collective-permute-start) | collective-permute-done | bytes 131104 | tf_op jit(solution)/shard_map/ppermute | solution.py:466
  103.9 1.0 pad_maximum_fusion.maps
  104.9 0.0 copy-done.3
  104.9 12.2 %shard_map.124 = f32[1024,1024]{1,0:T(8,128)} custom-call(s32[4,8,128]{2,1,0:T(8,128)S(1)} %copy-done.3, bf16[16,128,128]{2,1,0:T(8,128)(2,1)S(1)} %pad_maximum_fusion.maps), custom_call_target="tpu_custom_call" | custom-call | tf_op jit(solution)/shard_map/pallas_call | solution.py:445
  (2 shorter events, 0.0 us)
Async XLA Ops:
  0.6 40.4 %copy-start.4 = (f32[64]{0:T(128)S(1)}, f32[64]{0:T(128)}, u32[]{:S(2)}) copy-start(f32[64]{0:T(128)} %param.19) | copy-start | bytes 772
  0.6 40.4 %copy-start.5 = (f32[64]{0:T(128)S(1)}, f32[64]{0:T(128)}, u32[]{:S(2)}) copy-start(f32[64]{0:T(128)} %param.17) | copy-start | bytes 772
  0.7 40.3 %copy-start.6 = (f32[64]{0:T(128)S(1)}, f32[64]{0:T(128)}, u32[]{:S(2)}) copy-start(f32[64]{0:T(128)} %param.15) | copy-start | bytes 772
  6.1 2.2 %copy-start.1 = (f32[1024,1024]{1,0:T(8,128)S(1)}, f32[1024,1024]{1,0:T(8,128)}, u32[]{:S(2)}) copy-start(f32[1024,1024]{1,0:T(8,128)} %scan.1) | copy-start | bytes 12582916
  38.3 2.1 %copy-start = (bf16[1536,1536]{1,0:T(8,128)(2,1)}, bf16[1536,1536]{1,0:T(8,128)(2,1)S(1)}, u32[]{:S(2)}) copy-start(bf16[1536,1536]{1,0:T(8,128)(2,1)S(1)} %get-tuple-element.7.source) | copy-start | bytes 14155780
  40.4 0.6 copy-start.2
  41.0 63.9 %copy-start.3 = (s32[4,8,128]{2,1,0:T(8,128)S(1)}, s32[4,8,128]{2,1,0:T(8,128)}, u32[]{:S(2)}) copy-start(s32[4,8,128]{2,1,0:T(8,128)} %copy-done.2) | copy-start | bytes 49156
  91.4 9.6 %collective-permute-start.2 = (bf16[4,128,128]{2,1,0:T(8,128)(2,1)}, bf16[4,128,128]{2,1,0:T(8,128)(2,1)S(1)}, u32[]{:S(2)}, u32[]{:S(2)}) collective-permute-start(bf16[4,128,128]{2,1,0:T(8,128)(2,1)} %get-tuple-element.8), channel_id=1, source_target_pairs={{0,33},{1,34},{2,35},{3,36},{4,37},{5,38},{6,39},{7,40},{8,41},{9,... | collective-permute-start | bytes 393224 | tf_op jit(solution)/shard_map/ppermute | solution.py:466
  93.4 8.5 %collective-permute-start.1 = (bf16[4,128,128]{2,1,0:T(8,128)(2,1)}, bf16[4,128,128]{2,1,0:T(8,128)(2,1)S(1)}, u32[]{:S(2)}, u32[]{:S(2)}) collective-permute-start(bf16[4,128,128]{2,1,0:T(8,128)(2,1)} %get-tuple-element.8), channel_id=1, source_target_pairs={{0,32},{1,33},{2,34},{3,35},{4,36},{5,37},{6,38},{7,39},{8,40},{9,... | collective-permute-start | bytes 393224 | tf_op jit(solution)/shard_map/ppermute | solution.py:466
  95.3 8.6 %collective-permute-start = (bf16[4,128,128]{2,1,0:T(8,128)(2,1)}, bf16[4,128,128]{2,1,0:T(8,128)(2,1)S(1)}, u32[]{:S(2)}, u32[]{:S(2)}) collective-permute-start(bf16[4,128,128]{2,1,0:T(8,128)(2,1)} %get-tuple-element.8), channel_id=1, source_target_pairs={{0,1},{1,2},{2,3},{3,4},{4,5},{5,6},{6,7},{7,8},{8,9},{9,10},{10,1... | collective-permute-start | bytes 393224 | tf_op jit(solution)/shard_map/ppermute | solution.py:466

commit v3 on v2

--- a/solution.py
+++ b/solution.py
@@ -11,8 +11,8 @@
 C = 64
 F = 128
 SLOTS = 4
-BLOCKS = 16
-ROWS = 64
+BLOCKS = 32
+ROWS = 128
 LOW = -3.0e38
 MESH = pl.DeviceIdType.MESH
 WAYS = ((0, 0), (0, 1), (1, 0), (1, 1))
@@ -123,14 +123,14 @@
             jax.ShapeDtypeStruct((TILE + RIM, TILE + RIM), jnp.bfloat16),
             jax.ShapeDtypeStruct((4, 8, F), jnp.int32),
         ],
-        in_specs=[pl.BlockSpec(memory_space=pl.ANY), pl.BlockSpec(memory_space=pltpu.VMEM)],
-        out_specs=[pl.BlockSpec(memory_space=pl.ANY), pl.BlockSpec(memory_space=pltpu.VMEM)],
+        in_specs=[pl.BlockSpec(memory_space=pltpu.HBM), pl.BlockSpec(memory_space=pltpu.VMEM)],
+        out_specs=[pl.BlockSpec(memory_space=pltpu.HBM), pl.BlockSpec(memory_space=pltpu.VMEM)],
         scratch_shapes=[
             pltpu.VMEM((TILE, TILE), jnp.float32),
             pltpu.VMEM((TILE, TILE), jnp.bfloat16),
         ] + [pltpu.SemaphoreType.DMA((n,)) for n in sems],
         compiler_params=pltpu.CompilerParams(
-            collective_id=0, has_side_effects=True, vmem_limit_bytes=16 << 20
+            collective_id=0, has_side_effects=True, vmem_limit_bytes=60 << 20
         ),
     )(scan, own)
 
@@ -165,7 +165,8 @@
 
 
 def arrange(stem_raw, first_raw, second_raw, biases_raw, stem_w, first_w, second_w, back_w, biases):
-    turned = stem_raw[...].astype(jnp.float32).T.astype(jnp.bfloat16)
+    taps = [stem_raw[k // 7, k % 7].astype(jnp.float32) for k in range(49)]
+    turned = jnp.concatenate(taps, 0).T.astype(jnp.bfloat16)
     tap = lax.broadcasted_iota(jnp.int32, (49, 216), 0)
     tap_row, tap_col = tap // 7, tap % 7
     place_col, place_row = lanes((49, 216)) // 24, lanes((49, 216)) % 24
@@ -227,7 +228,8 @@
         stem_raw, first_raw, second_raw, biases_raw, stem_w, first_w, second_w, back_w, biases
     )
     map_ref[...] = jnp.zeros_like(map_ref)
-    logit_ref[...] = jnp.zeros_like(logit_ref)
+    for slot in range(SLOTS):
+        logit_ref[slot] = jnp.float32(0.0)
 
     def window(number, _):
         slot, top, left, target = place(number)
@@ -292,8 +294,11 @@
 
         convolved(feats, first_w, after_first)
 
-        head = jnp.where(lanes((C, 9)) == target, heads[...].astype(jnp.float32), 0.0)
-        column = jnp.sum(head, 1, keepdims=True)
+        eye = lax.broadcasted_iota(jnp.int32, (C, C), 0) == lanes((C, C))
+        wanted = lax.broadcasted_iota(jnp.int32, (9, C), 0) == target
+        head = jnp.where(wanted, heads[...].astype(jnp.float32), 0.0)
+        head = jnp.sum(head, 0, keepdims=True)
+        column = jnp.sum(jnp.where(eye, head, 0.0), 1, keepdims=True)
         grad = jnp.broadcast_to(
             (column / float(F * F)).astype(jnp.bfloat16).astype(jnp.float32), (C, F)
         )
@@ -325,12 +330,11 @@
         mean = jnp.sum(acc[0], 1, keepdims=True) / float(F * F)
         logit = jnp.sum(mean * column)
         bias = jnp.sum(jnp.where(lanes((1, 9)) == target, head_bias[...], 0.0))
-        logit_ref[slot] = jnp.full((8, F), logit + bias, jnp.float32)
+        logit_ref[slot] = logit + bias
 
         whole = acc[2]
         parts = [whole - acc[4], whole, whole - acc[3]]
         lane = lanes((C, F))
-        eye = lax.broadcasted_iota(jnp.int32, (C, C), 0) == lanes((C, C))
         channel = jnp.sum(acc[1], 1, keepdims=True)
         for dy in range(3):
             for dx in range(3):
@@ -365,9 +369,9 @@
     whole = pl.BlockSpec(memory_space=pltpu.VMEM)
     maps, logits = pl.pallas_call(
         net_kernel,
-        in_specs=[pl.BlockSpec(memory_space=pltpu.SMEM), pl.BlockSpec(memory_space=pl.ANY)]
+        in_specs=[pl.BlockSpec(memory_space=pltpu.SMEM), pl.BlockSpec(memory_space=pltpu.HBM)]
         + [whole] * 6,
-        out_specs=[whole, whole],
+        out_specs=[whole, pl.BlockSpec(memory_space=pltpu.SMEM)],
         scratch_shapes=[
             pltpu.VMEM((16 * C, 216), jnp.bfloat16),
             pltpu.VMEM((3 * C, 3 * C), jnp.bfloat16),
@@ -386,14 +390,14 @@
         ],
         out_shape=[
             jax.ShapeDtypeStruct((SLOTS, F, F), jnp.bfloat16),
-            jax.ShapeDtypeStruct((SLOTS, 8, F), jnp.float32),
+            jax.ShapeDtypeStruct((SLOTS,), jnp.float32),
         ],
         compiler_params=pltpu.CompilerParams(vmem_limit_bytes=58 << 20),
     )(
-        infos, framed, stem_weight.reshape(49, C), conv1_weight.reshape(9, C, C),
-        conv2_weight.reshape(9, C, C), biases, head_weight, head_bias.reshape(1, 9),
+        infos, framed, stem_weight, conv1_weight.reshape(9, C, C),
+        conv2_weight.reshape(9, C, C), biases, head_weight.T, head_bias.reshape(1, 9),
     )
-    return maps, logits[:, 0, 0]
+    return maps, logits
 
 
 def blend_kernel(infos, maps, out_ref, total):
@@ -426,7 +430,7 @@
             in_col = (col >= 0) & (col < WIN)
             side = jnp.where(in_col, profile(col.astype(jnp.float32)), 0.0)[0:1]
             tall = jnp.dot(
-                up.astype(jnp.bfloat16), maps[number], preferred_element_type=jnp.float32
+                up.astype(jnp.bfloat16), maps[way, slot], preferred_element_type=jnp.float32
             ).astype(jnp.bfloat16)
             for k in range(5):
                 part = slice(k * F, (k + 1) * F)
@@ -455,15 +459,54 @@
     )(infos, maps)
 
 
-def moved(shard, down, right):
+def share_kernel(maps, every, keep, send, recv):
+    row, col = lax.axis_index("row"), lax.axis_index("col")
     rows, cols = lax.axis_size("row"), lax.axis_size("col")
-    pairs = [
-        (r * cols + c, (r + down) * cols + c + right)
-        for r in range(rows)
-        for c in range(cols)
-        if 0 <= r + down < rows and 0 <= c + right < cols
-    ]
-    return lax.ppermute(shard, ("row", "col"), pairs)
+    up, down, left, right = row > 0, row < rows - 1, col > 0, col < cols - 1
+    own = pltpu.make_async_copy(maps, every.at[0], keep)
+    own.start()
+    goes = (right, down, down & right)
+    comes = (left, up, up & left)
+    barrier = pltpu.get_barrier_semaphore()
+    for (by_row, by_col), out, back in zip(WAYS[1:], goes, comes):
+        for sign, there in ((1, out), (-1, back)):
+            @pl.when(there)
+            def _():
+                pl.semaphore_signal(
+                    barrier, inc=1, device_id=(row + sign * by_row, col + sign * by_col),
+                    device_id_type=MESH,
+                )
+    pl.semaphore_wait(barrier, sum(there.astype(jnp.int32) for there in goes + comes))
+    copies = [
+        pltpu.make_async_remote_copy(
+            src_ref=maps, dst_ref=every.at[k], send_sem=send.at[k - 1], recv_sem=recv.at[k - 1],
+            device_id=(row + WAYS[k][0], col + WAYS[k][1]), device_id_type=MESH,
+        )
+        for k in (1, 2, 3)
+    ]
+    for k in (2, 1, 0):
+        pl.when(goes[k])(copies[k].start)
+    own.wait()
+    for k in range(3):
+        pl.when(goes[k])(copies[k].wait_send)
+        pl.when(comes[k])(copies[k].wait_recv)
+
+
+def share(maps):
+    return pl.pallas_call(
+        share_kernel,
+        out_shape=jax.ShapeDtypeStruct((4,) + maps.shape, maps.dtype),
+        in_specs=[pl.BlockSpec(memory_space=pltpu.VMEM)],
+        out_specs=pl.BlockSpec(memory_space=pltpu.VMEM),
+        scratch_shapes=[
+            pltpu.SemaphoreType.DMA,
+            pltpu.SemaphoreType.DMA((3,)),
+            pltpu.SemaphoreType.DMA((3,)),
+        ],
+        compiler_params=pltpu.CompilerParams(
+            collective_id=1, has_side_effects=True, vmem_limit_bytes=40 << 20
+        ),
+    )(maps)
 
 
 def local(scan, anchors, targets, *network):
@@ -471,8 +514,7 @@
     own = jnp.pad(own, ((0, 8 - SLOTS), (0, F - 3)), constant_values=-1)
     framed, infos = frame(scan, own)
     maps, scores = networks(infos, framed, *network)
-    every = jnp.concatenate([maps] + [moved(maps, *way) for way in WAYS[1:]], 0)
-    saliency = blend(infos, every)
+    saliency = blend(infos, share(maps))
     return saliency, scores.reshape(targets.shape)
 
 

time: 118 us -> 111 us (0.941)
  the two profiles are of different devices: /device:TPU:70 before, /device:TPU:36 now
where the time goes in v3:
time: 111 us; the launch traced here: 109 us
  Pallas kernels  101 us (91%)
  local copies, waits for them, and re-layouts  4.7 us (4%)
  other arithmetic  3.37 us (3%)
    pallas_call x1, Pallas kernels, share(): pl.pallas_call(share_kernel, out_shape=jax.ShapeDtypeStruct((4,) + maps.s...  45.9 us
    pallas_call x1, Pallas kernels, frame(): pl.pallas_call(frame_kernel, out_shape=[jax.ShapeDtypeStruct((TILE + RIM,...  32.8 us
    pallas_call x1, Pallas kernels, networks(): pl.pallas_call(net_kernel, in_specs=[pl.BlockSpec(memory_space=pltpu.SMEM...  15.4 us
    pallas_call x1, Pallas kernels, blend(): pl.pallas_call(blend_kernel, in_specs=[pl.BlockSpec(memory_space=pltpu.SM...  6.62 us
    unnamed x6, local copies, waits for them, and re-layouts  2.75 us

profile of v3, /device:TPU:36, one launch (start us, length us, event | category | flops | bytes accessed | tf_op | source)
XLA Modules:
  0.0 109.4 jit_solution(8201622220839326532)
XLA Ops:
  0.6 0.5 broadcast.5
  1.1 1.3 %reduce.3 = s32[2,2]{1,0:T(2,128)S(1)} reduce(s32[2,2,1]{1,2,0:T(1,128)} %param.13, s32[]{:T(128)} %broadcast.5), dimensions={2}, to_apply=%param.13.reduce_sub_computation.3 | reduce | bytes 36 | tf_op args[2]
  2.5 0.1 reshape.28
  2.6 0.8 pad_add_fusion
  3.3 0.6 pad.4.own
  3.9 1.3 %pad_maximum_fusion.biases_raw = f32[3,64]{1,0:T(4,128)} fusion(f32[1,64]{1,0:T(1,128)} %bitcast.15, f32[1,64]{1,0:T(1,128)} %bitcast.16, f32[1,64]{1,0:T(1,128)} %bitcast.17), kind=kLoop, calls=%fused_computation.1 | loop fusion | flops 384 | bytes 1536 | tf_op jit(solution)/shard_map/stack | solution.py:368
  5.2 1.3 %copy.16.stem_raw = bf16[7,7,1,64]{3,2,1,0:T(2,128)(2,1)} copy(bf16[7,7,1,64]{3,1,2,0:T(8,128)(2,1)} %param.14) | data formatting | bytes 12544 | tf_op args[3]
  6.5 32.8 %shard_map.122 = (bf16[1536,1536]{1,0:T(8,128)(2,1)}, s32[4,8,128]{2,1,0:T(8,128)}) custom-call(f32[1024,1024]{1,0:T(8,128)} %scan.1, s32[8,128]{1,0:T(8,128)} %pad.4.own), custom_call_target="tpu_custom_call" | custom-call | tf_op jit(solution)/shard_map/pallas_call | solution.py:120
  39.3 0.0 copy-start.1
  39.3 15.4 %shard_map.123 = (bf16[4,128,128]{2,1,0:T(8,128)(2,1)}, f32[4]{0:T(128)}) custom-call(s32[4,8,128]{2,1,0:T(8,128)} %get-tuple-element.6.infos, bf16[1536,1536]{1,0:T(8,128)(2,1)} %get-tuple-element.7.source, bf16[7,7,1,64]{3,2,1,0:T(2,128)(2,1)} %copy.16.stem_raw, bf16[9,64,64]{2,1,0:T(8,128)(2,1)} %bitcast.10, bf16[9,64,64]{2,1,0:T(8,128)(2,1)} %bitcast.11, ...), custom_call_target="tpu_custom_call" | custom-call | tf_op jit(solution)/shard_map/pallas_call | solution.py:370
  54.7 1.3 %reshape.27 = f32[2,2,1]{1,0,2:T(2,128)} reshape(f32[4]{0:T(128)} %get-tuple-element.9) | data formatting | bytes 32 | tf_op jit(solution)/shard_map/reshape | solution.py:518
  56.0 0.0 copy-start
  56.0 0.9 copy-done
  56.9 45.9 %shard_map.124.maps = bf16[4,4,128,128]{3,2,1,0:T(8,128)(2,1)S(1)} custom-call(bf16[4,128,128]{2,1,0:T(8,128)(2,1)S(1)} %copy-done), custom_call_target="tpu_custom_call" | custom-call | tf_op jit(solution)/shard_map/pallas_call | solution.py:496
  102.8 0.0 copy-done.1
  102.8 6.6 %shard_map.125 = f32[1024,1024]{1,0:T(8,128)} custom-call(s32[4,8,128]{2,1,0:T(8,128)S(1)} %copy-done.1, bf16[4,4,128,128]{3,2,1,0:T(8,128)(2,1)S(1)} %shard_map.124.maps), custom_call_target="tpu_custom_call" | custom-call | tf_op jit(solution)/shard_map/pallas_call | solution.py:449
Async XLA Ops:
  39.3 63.5 %copy-start.1 = (s32[4,8,128]{2,1,0:T(8,128)S(1)}, s32[4,8,128]{2,1,0:T(8,128)}, u32[]{:S(2)}) copy-start(s32[4,8,128]{2,1,0:T(8,128)} %get-tuple-element.6.infos) | copy-start | bytes 49156
  56.0 0.9 copy-start
